TPU v7x, 512 devices: a whole 4x8x8 slice. The times are simulated.
512 devices in a mesh: frame: 32 (over x, z_lo, core), batch: 16 (over z_hi, y).
Axes of the slice: x: 4, y: 8, z: 8 (z_hi: 2, z_lo: 4; z = z_hi * 4 + z_lo), core: 2. Of those that a mesh axis runs over, the one named last changes fastest.
Arguments:
- window: float32 [262144, 128], P(('batch', 'frame')), parts along dimension 0, may hold values from -6 to 6
- noise: float32 [262144, 2, 128], P(('batch', 'frame')), parts along dimension 0, may hold values from -6 to 6
- fresh: float32 [8192, 128], P('batch'), parts along dimension 0, may hold values from -12 to 12
- levels: int32 [512, 2], P(('batch', 'frame')), parts along dimension 0, may hold values from 0 to 31
- reach: int32 [512], P('batch'), parts along dimension 0, may hold values from 1 to 31
- w_in: bfloat16 [128, 1024], replicated, may hold values from -0.5 to 0.5
- w_level: bfloat16 [256, 1024], replicated, may hold values from -0.375 to 0.375
- norm_gain: float32 [1024], replicated, may hold values from 0.25 to 1.75
- w_qkv: bfloat16 [1024, 3072], P('frame'), as said below
- w_out: bfloat16 [1024, 128], replicated, may hold values from -0.1875 to 0.1875
- w_res: bfloat16 [1024, 128], replicated, may hold values from -0.1875 to 0.1875
Outputs:
- final_window: float32 [262144, 128], P(('batch', 'frame')), parts along dimension 0
There are 16 independent parts, one for each index of `batch`. A program takes and returns all parts, laid end to end along the dimension named above; an argument that names none is the same for every part. Nothing has to cross between parts.
Inputs may be any that keep to these rules, and one draw needn't show every extreme that they name: `w_qkv`: projection weights of fan-in 1024.
All inputs are finite; a program needn't handle non-finite values.
Results may differ from a plain program's by a relative error of at most 0.017.
Values may be sent and summed in bfloat16 or wider, within the bound.
No kernel may reach another device: no remote copies, remote signals or barrier semaphores. Data moves between devices by JAX's collectives and lax.ppermute only.
A program may use at most 64 MiB of HBM per device.

v0:
```python
import math

import jax
import jax.numpy as jnp
from jax import lax
from jax.sharding import PartitionSpec as P

HEADS = 8
HDIM = 128
FREQ = 128
PASSES = 2
LEVELS = 32


def shifted(block, axis, distance):
    devices = range(lax.axis_size(axis))
    route = [(i - distance, i) for i in devices if i - distance in devices]
    return lax.ppermute(block, axis, route)


def sigma_of(level):
    return 4.0 * jnp.exp(level.astype(jnp.float32) * jnp.float32(math.log(1.0 / 16.0) / LEVELS))


def level_feats(level):
    sigma = sigma_of(level)
    index = jnp.arange(FREQ).astype(jnp.float32)
    freqs = jnp.exp(index * jnp.float32(math.log(100.0) / FREQ))
    angle = jnp.log(sigma) * freqs[None, :]
    return jnp.concatenate([jnp.sin(angle), jnp.cos(angle)], axis=1).astype(jnp.bfloat16)


def attention(block, reach):
    frames, count = (block.shape[0], block.shape[1])
    width = HEADS * HDIM
    query = block[:, :, :width].reshape(frames, count, HEADS, HDIM)
    keys = block[:, :, width : 2 * width].reshape(frames, count, HEADS, HDIM)
    values = block[:, :, 2 * width :].reshape(frames, count, HEADS, HDIM)
    scores = jnp.einsum("fnhd,gnhd->nhfg", query, keys, preferred_element_type=jnp.float32)
    scores = scores / jnp.float32(math.sqrt(HDIM))
    slots = jnp.arange(frames)
    allowed = (slots[None, :] <= slots[:, None]) & (
        slots[None, :] >= slots[:, None] - reach[:, None]
    )
    scores = jnp.where(allowed[None, None], scores, jnp.float32(-1e30))
    top = jnp.max(scores, axis=-1, keepdims=True)
    expo = jnp.exp(scores - top)
    probs = (expo / jnp.sum(expo, axis=-1, keepdims=True)).astype(jnp.bfloat16)
    result = jnp.einsum("nhfg,gnhd->fnhd", probs, values, preferred_element_type=jnp.float32)
    return result.astype(jnp.bfloat16).reshape(frames, count, width)


def return_rows(blocks):
    back = lax.all_to_all(blocks, "frame", split_axis=0, concat_axis=0, tiled=True)
    return back.reshape(back.shape[0] * back.shape[1], back.shape[2])


def attend_projected(qkv_rows, reach, frames):
    split_rows = qkv_rows.reshape(frames, qkv_rows.shape[0] // frames, qkv_rows.shape[1])
    blocks = attention(
        lax.all_to_all(split_rows, "frame", split_axis=0, concat_axis=0, tiled=True), reach
    )
    return return_rows(blocks)


def on_device(window, noise, fresh, levels, reach, w_in, w_level, norm_gain, w_qkv, w_out, w_res):
    frames = lax.axis_size("frame")
    place = lax.axis_index("frame")
    state = window
    full_weights = lax.all_gather(w_qkv, "frame", axis=0, tiled=True)
    for step in range(PASSES):
        level = levels[0, step]
        sigma = sigma_of(level)
        sigma_next = sigma_of(level + 1)
        scaled = (state / jnp.sqrt(1.0 + sigma * sigma)).astype(jnp.bfloat16)
        embed = jnp.dot(
            level_feats(level.reshape(1, 1)), w_level, preferred_element_type=jnp.float32
        )
        hidden = jnp.dot(scaled, w_in, preferred_element_type=jnp.float32) + embed
        normed = (
            hidden
            * lax.rsqrt(jnp.mean(hidden * hidden, axis=-1, keepdims=True) + 1e-06)
            * norm_gain
        )
        normed = normed.astype(jnp.bfloat16)
        qkv_rows = jnp.dot(normed, full_weights, preferred_element_type=jnp.float32).astype(
            jnp.bfloat16
        )
        attn = attend_projected(qkv_rows, reach, frames)
        pred = jnp.dot(attn, w_out, preferred_element_type=jnp.float32) + jnp.dot(
            normed, w_res, preferred_element_type=jnp.float32
        )
        state = state - sigma * pred + sigma_next * (0.8 * pred + 0.6 * noise[:, step, :])
        if step + 1 < PASSES:
            moved = shifted(state, "frame", -1)
            state = jnp.where(place == frames - 1, fresh, moved)
    return state


def solution(mesh):
    return jax.shard_map(
        on_device,
        mesh=mesh,
        in_specs=(
            P(("batch", "frame"), None),
            P(("batch", "frame"), None, None),
            P("batch", None),
            P(("batch", "frame"), None),
            P("batch"),
            P(),
            P(),
            P(),
            P("frame", None),
            P(),
            P(),
        ),
        out_specs=P(("batch", "frame"), None),
        check_vma=False,
    )
```

profile of v0, /device:TPU:1, one launch (start us, length us, event | category | flops | bytes accessed | tf_op | source)
XLA Modules:
  0.0 377.4 jit_solution(12198338753556861352)
XLA Ops:
  11.2 73.7 %all-gather.2.cloned.1.call-done = bf16[1024,3072]{1,0:T(8,128)(2,1)} async-done(((bf16[32,3072]{1,0:T(8,128)(2,1)}), bf16[1024,3072]{1,0:T(8,128)(2,1)}) %all-gather.2.cloned.1.call-update) | async-done | bytes 6291472 | tf_op jit(solution)/shard_map/all_gather | solution.py:70
  84.9 7.7 %convolution_convert_fusion.1 = bf16[512,3072]{1,0:T(8,128)(2,1)} fusion(bf16[1024,3072]{1,0:T(8,128)(2,1)} %all-gather.2.cloned.1.call-done, f32[512,1024]{1,0:T(8,128)S(1)} %get-tuple-element.16, f32[1024]{0:T(1024)S(1)} %copy-done.5, f32[512]{0:T(512)S(1)} %add_rsqrt_fusion.1, f32[1024]{0:T(1024)S(1)} %bitcast.91), kind=kOutput, calls=%fused_computation.3 | convolution fusion | flops 3224895488 | bytes 11544576 | tf_op jit(solution)/shard_map/dot_general | solution.py:86
  92.6 5.6 %all-to-all-start = ((bf16[32,16,3072]{2,1,0:T(8,128)(2,1)}), bf16[32,16,3072]{2,1,0:T(8,128)(2,1)}, u32[]{:S(2)}, u32[]{:S(2)}) async-start(bf16[32,16,3072]{2,1,0:T(8,128)(2,1)} %bitcast.80), calls=%async_computation | async-start | bytes 6291456 | tf_op jit(solution)/shard_map/all_to_all | solution.py:61
  98.3 72.0 %all-to-all-done = bf16[32,16,3072]{2,1,0:T(8,128)(2,1)} async-done(((bf16[32,16,3072]{2,1,0:T(8,128)(2,1)}), bf16[32,16,3072]{2,1,0:T(8,128)(2,1)}, u32[]{:S(2)}, u32[]{:S(2)}) %all-to-all-start) | async-done | bytes 3145760 | tf_op jit(solution)/shard_map/all_to_all | solution.py:61
  170.3 2.2 fusion.62
  176.3 4.8 %fusion.65 = (f32[16,8,32]{2,1,0:T(8,128)S(1)}, f32[16,8,32,32]{2,3,1,0:T(8,128)}) fusion(pred[32,32]{0,1:T(8,128)(4,1)S(1)} %fusion.30, bf16[32,16,8,128]{3,2,1,0:T(8,128)(2,1)} %bitcast.86, bf16[32,16,8,128]{3,2,1,0:T(8,128)(2,1)} %bitcast.83), kind=kOutput, calls=%fused_computation.74 | convolution fusion | flops 34078752 | bytes 2638848 | tf_op jit(solution)/shard_map/sub | solution.py:47
  181.1 2.9 fusion.4
  185.4 2.3 reshape.162
  187.7 5.6 %all-to-all-start.1 = ((bf16[32,16,1024]{2,1,0:T(8,128)(2,1)}), bf16[32,16,1024]{2,1,0:T(8,128)(2,1)}, u32[]{:S(2)}, u32[]{:S(2)}) async-start(bf16[32,16,1024]{2,1,0:T(8,128)(2,1)} %reshape.162), calls=%async_computation.1 | async-start | bytes 2097152 | tf_op jit(solution)/shard_map/all_to_all | solution.py:54
  194.7 2.5 fusion.63
  197.2 24.1 %all-to-all-done.1 = bf16[32,16,1024]{2,1,0:T(8,128)(2,1)} async-done(((bf16[32,16,1024]{2,1,0:T(8,128)(2,1)}), bf16[32,16,1024]{2,1,0:T(8,128)(2,1)}, u32[]{:S(2)}, u32[]{:S(2)}) %all-to-all-start.1) | async-done | bytes 1048608 | tf_op jit(solution)/shard_map/all_to_all | solution.py:54
  221.3 1.7 fusion.76
  223.0 2.3 fusion.25
  225.2 2.2 collective-permute-start
  227.7 5.4 %collective-permute-done = f32[512,128]{1,0:T(8,128)S(1)} collective-permute-done((f32[512,128]{1,0:T(8,128)}, f32[512,128]{1,0:T(8,128)S(1)}, u32[]{:S(2)}, u32[]{:S(2)}) %collective-permute-start) | collective-permute-done | bytes 262176 | tf_op jit(solution)/shard_map/ppermute | solution.py:18
  233.6 6.6 %convolution_convert_fusion = bf16[512,3072]{1,0:T(8,128)(2,1)S(1)} fusion(bf16[1024,3072]{1,0:T(8,128)(2,1)} %all-gather.2.cloned.1.call-done, f32[512,1024]{1,0:T(8,128)S(1)} %get-tuple-element.20, f32[512]{0:T(512)S(1)} %add_rsqrt_fusion, f32[1024]{0:T(1024)S(1)} %bitcast.94, f32[1024]{0:T(1024)S(1)} %copy-done.5), kind=kOutput, calls=%fused_computation.2 | convolution fusion | flops 3224895488 | bytes 11544576 | tf_op jit(solution)/shard_map/dot_general | solution.py:86
  240.2 78.0 %all_to_all.20 = bf16[32,16,3072]{2,1,0:T(8,128)(2,1)S(1)} all-to-all(bf16[32,16,3072]{2,1,0:T(8,128)(2,1)S(1)} %bitcast.81), channel_id=1, replica_groups=mesh['frame'=32,'batch'=16] {'frame'}, dimensions={0} | all-to-all | bytes 6291456 | tf_op jit(solution)/shard_map/all_to_all | solution.py:61
  322.5 4.8 %fusion.70 = (f32[16,8,32]{2,1,0:T(8,128)S(1)}, f32[16,8,32,32]{2,3,1,0:T(8,128)}) fusion(pred[32,32]{0,1:T(8,128)(4,1)S(1)} %fusion.30, bf16[32,16,8,128]{3,2,1,0:T(8,128)(2,1)} %bitcast.84, bf16[32,16,8,128]{3,2,1,0:T(8,128)(2,1)} %bitcast.82), kind=kOutput, calls=%fused_computation.75 | convolution fusion | flops 34078752 | bytes 2638848 | tf_op jit(solution)/shard_map/sub | solution.py:47
  327.3 2.9 fusion.5
  331.6 2.3 reshape.168
  333.9 4.7 %all-to-all-start.3 = ((bf16[32,16,1024]{2,1,0:T(8,128)(2,1)}), bf16[32,16,1024]{2,1,0:T(8,128)(2,1)}, u32[]{:S(2)}, u32[]{:S(2)}) async-start(bf16[32,16,1024]{2,1,0:T(8,128)(2,1)} %reshape.168), calls=%async_computation.3 | async-start | bytes 2097152 | tf_op jit(solution)/shard_map/all_to_all | solution.py:54
  339.3 27.4 %all-to-all-done.3 = bf16[32,16,1024]{2,1,0:T(8,128)(2,1)} async-done(((bf16[32,16,1024]{2,1,0:T(8,128)(2,1)}), bf16[32,16,1024]{2,1,0:T(8,128)(2,1)}, u32[]{:S(2)}, u32[]{:S(2)}) %all-to-all-start.3) | async-done | bytes 1048608 | tf_op jit(solution)/shard_map/all_to_all | solution.py:54
  366.6 1.7 fusion.78
  368.3 2.2 fusion.23
  (40 shorter events, 15.6 us)
Async XLA Ops:
  6.5 2.9 copy-start
  6.5 78.3 %copy-start.5 = (f32[1024]{0:T(1024)S(1)}, f32[1024]{0:T(1024)}, u32[]{:S(2)}) copy-start(f32[1024]{0:T(1024)} %param.18) | copy-start | bytes 12292
  6.5 78.3 %all-gather.2.cloned.1.call-start = ((), (), s32[]{:S(2)}) async-start(), calls=%async_computation.4 | async-start | bytes 6488064 | tf_op jit(solution)/shard_map/all_gather | solution.py:70
  92.6 5.6 %copy-start.6 = (s32[32]{0:T(128)S(1)}, s32[32]{0:T(128)}, u32[]{:S(2)}) copy-start(s32[32]{0:T(128)} %param.15) | copy-start | bytes 388
  92.6 77.7 %all-to-all-start = ((bf16[32,16,3072]{2,1,0:T(8,128)(2,1)}), bf16[32,16,3072]{2,1,0:T(8,128)(2,1)}, u32[]{:S(2)}, u32[]{:S(2)}) async-start(bf16[32,16,3072]{2,1,0:T(8,128)(2,1)} %bitcast.80), calls=%async_computation | async-start | bytes 6291456 | tf_op jit(solution)/shard_map/all_to_all | solution.py:61
  187.7 33.6 %copy-start.3 = (bf16[1024,128]{1,0:T(8,128)(2,1)S(1)}, bf16[1024,128]{1,0:T(8,128)(2,1)}, u32[]{:S(2)}) copy-start(bf16[1024,128]{1,0:T(8,128)(2,1)} %param.20) | copy-start | bytes 786436
  187.7 35.3 %copy-start.2 = (f32[512,128]{1,0:T(8,128)S(1)}, f32[512,128]{1,0:T(8,128)}, u32[]{:S(2)}) copy-start(f32[512,128]{1,0:T(8,128)} %param.11) | copy-start | bytes 786436
  187.7 33.6 %all-to-all-start.1 = ((bf16[32,16,1024]{2,1,0:T(8,128)(2,1)}), bf16[32,16,1024]{2,1,0:T(8,128)(2,1)}, u32[]{:S(2)}, u32[]{:S(2)}) async-start(bf16[32,16,1024]{2,1,0:T(8,128)(2,1)} %reshape.162), calls=%async_computation.1 | async-start | bytes 2097152 | tf_op jit(solution)/shard_map/all_to_all | solution.py:54
  222.9 10.2 %copy-start.1 = (bf16[128,1024]{1,0:T(8,128)(2,1)S(1)}, bf16[128,1024]{1,0:T(8,128)(2,1)}, u32[]{:S(2)}) copy-start(bf16[128,1024]{1,0:T(8,128)(2,1)} %param.16) | copy-start | bytes 786436
  225.2 7.9 %collective-permute-start = (f32[512,128]{1,0:T(8,128)}, f32[512,128]{1,0:T(8,128)S(1)}, u32[]{:S(2)}, u32[]{:S(2)}) collective-permute-start(f32[512,128]{1,0:T(8,128)} %fusion.25), channel_id=1, source_target_pairs={{16,0},{32,16},{48,32},{64,48},{80,64},{96,80},{112,96},{128,112},... | collective-permute-start | bytes 786440 | tf_op jit(solution)/shard_map/ppermute | solution.py:18
  333.9 34.4 %copy-start.4 = (f32[512,128]{1,0:T(8,128)S(1)}, f32[512,128]{1,0:T(8,128)}, u32[]{:S(2)}) copy-start(f32[512,128]{1,0:T(8,128)} %param.13) | copy-start | bytes 786436
  333.9 32.7 %all-to-all-start.3 = ((bf16[32,16,1024]{2,1,0:T(8,128)(2,1)}), bf16[32,16,1024]{2,1,0:T(8,128)(2,1)}, u32[]{:S(2)}, u32[]{:S(2)}) async-start(bf16[32,16,1024]{2,1,0:T(8,128)(2,1)} %reshape.168), calls=%async_computation.3 | async-start | bytes 2097152 | tf_op jit(solution)/shard_map/all_to_all | solution.py:54
Sparse Core Ops, SparseCore 0:
  9.5 75.3 all-gather.1
where the time goes:
time: 378 us; the launch traced here: 377 us
  waiting for transfers between devices  203 us (54%)
  blocking collectives  78 us (21%)
  matrix products  39.8 us (11%)
  local copies, waits for them, and re-layouts  21.5 us (6%)
  starting transfers between devices  18.1 us (5%)
  between operations  16.5 us (4%)
    all_to_all x1, blocking collectives, attend_projected(): lax.all_to_all(split_rows, 'frame', split_axis=0, concat_axis=0, tiled=True)  78 us
    all_gather x1, waiting for transfers between devices, on_device(): full_weights = lax.all_gather(w_qkv, 'frame', axis=0, tiled=True)  73.7 us
    all_to_all x1, waiting for transfers between devices, attend_projected(): lax.all_to_all(split_rows, 'frame', split_axis=0, concat_axis=0, tiled=True)  72 us
    all_to_all x2, waiting for transfers between devices, return_rows(): lax.all_to_all(blocks, 'frame', split_axis=0, concat_axis=0, tiled=True)  51.5 us
    dot_general x2, matrix products, on_device(): jnp.dot(normed, full_weights, preferred_element_type=jnp.float32)  14.3 us
    all_to_all x2, starting transfers between devices, return_rows(): lax.all_to_all(blocks, 'frame', split_axis=0, concat_axis=0, tiled=True)  10.3 us
    sub x2, matrix products, attention(): expo = jnp.exp(scores - top)  9.58 us
    unnamed x20, local copies, waits for them, and re-layouts  7.63 us
  transfers between devices with their start and end apart: 5, of which 5 were waited for; matrix products, arithmetic and copies ran while one was open for 2% of the time, Pallas kernels for 0%

commit v1 on v0

v1 whole, which is shorter than its diff:
```python
import math

import jax
import jax.numpy as jnp
import numpy as np
from jax import lax
from jax.experimental import pallas as pl
from jax.experimental.pallas import tpu as pltpu
from jax.sharding import PartitionSpec as P

HEADS = 8
HDIM = 128
C = 128
D = 1024
FREQ = 128
LEVELS = 32
FRAMES = 32
ROWS = 512
POS = ROWS // FRAMES
GROUP = 8
SPAN = FRAMES * GROUP
PART = 32
DECAY = math.log(1.0 / 16.0) / LEVELS
BF16 = jnp.bfloat16
F32 = jnp.float32
VMEM = pl.BlockSpec(memory_space=pltpu.VMEM)
SMEM = pl.BlockSpec(memory_space=pltpu.SMEM)


def sigma_of(level):
    return 4.0 * jnp.exp(level * F32(DECAY))


def feats_table():
    sigma = 4.0 * np.exp(np.arange(LEVELS) * DECAY)
    freqs = np.exp(np.arange(FREQ) * (math.log(100.0) / FREQ))
    angle = np.log(sigma)[:, None] * freqs[None, :]
    return jnp.asarray(np.concatenate([np.sin(angle), np.cos(angle)], axis=1), F32).astype(BF16)


def dot(a, b):
    return jnp.dot(a, b, preferred_element_type=F32)


def iota(shape, dim):
    return lax.broadcasted_iota(jnp.int32, shape, dim)


def pack_kernel(levels, window, noise, w_qkv, out, base_out, late_out):
    first = jnp.full((8, C), levels[0, 0], jnp.int32).astype(F32)
    second = jnp.full((8, C), levels[0, 1], jnp.int32).astype(F32)
    sigma = sigma_of(first)[:1]
    state = window[...]
    scaled = state / jnp.sqrt(1.0 + sigma * sigma)
    base = state + (0.6 * sigma_of(first + 1.0)[:1]) * noise[pl.ds(0, ROWS, stride=2), :]
    base_out[...] = base
    late_out[...] = (0.6 * sigma_of(second + 1.0)[:1]) * noise[pl.ds(1, ROWS, stride=2), :]
    out[:, 32:48, :] = scaled.reshape(FRAMES, POS, C).astype(BF16)
    out[:, 48:64, :] = base.reshape(FRAMES, POS, C).astype(BF16)
    row = iota((3 * HDIM, 1), 0)
    target = (row % HDIM) // PART * HDIM + row // HDIM * PART + row % PART
    pick = (iota((3 * HDIM, 4 * HDIM), 1) == target).astype(F32).astype(BF16)
    stacked = jnp.concatenate(
        [
            jnp.concatenate(
                [w_qkv[:, s * D + h * HDIM : s * D + (h + 1) * HDIM] for s in range(3)], axis=1
            )
            for h in range(HEADS)
        ],
        axis=0,
    )
    pieces = dot(stacked, pick)
    lane = iota((PART, HDIM), 1)
    for h in range(HEADS):
        for i in range(4):
            piece = pieces[h * PART : (h + 1) * PART, i * HDIM : (i + 1) * HDIM]
            piece = jnp.where(lane == 96, first[:1], jnp.where(lane == 97, second[:1], piece))
            out[4 * h + i, 0:32, :] = piece.astype(BF16)


def table_kernel(feats, w_level, w_in, gain, high, low, embed_in):
    emb = dot(feats[...], w_level[...])
    emb_high = emb.astype(BF16)
    embed_in[0:128, :] = w_in[...]
    embed_in[128:160, :] = emb_high
    embed_in[160:192, :] = (emb - emb_high.astype(F32)).astype(BF16)
    embed_in[192:256, :] = jnp.zeros((64, D), BF16)
    scaled = jnp.concatenate([w_in[...].astype(F32), emb], axis=0) * gain[...]
    top = scaled.astype(BF16)
    high[...] = top
    low[...] = (scaled - top.astype(F32)).astype(BF16)


def project_kernel(received, high, low, out):
    part = received[:, 0:32, :].reshape(D, HDIM)
    product = dot(high[...], part) + dot(low[...], part)
    emb = product[128:160]
    beside = jnp.concatenate(
        [pltpu.roll(emb, 96, 1), pltpu.roll(emb, 64, 1), pltpu.roll(emb, 32, 1), jnp.zeros_like(emb)],
        axis=0,
    )
    packed = jnp.where(iota((C, HDIM), 1) < 96, product[:128], beside).astype(BF16)
    out[...] = jnp.broadcast_to(packed[None], out.shape)


def passes_kernel(
    place, reach, received, mine, other, embed_in, gain, w_out, w_res, fresh, out, proj, attn
):
    core = place[0] % 2
    row = iota((4 * HDIM, 1), 0)
    piece = row // HDIM
    target = row % HDIM // PART * HDIM + (piece + core - 2 * (piece % 2) * core) * PART + row % PART
    pick = (iota((4 * HDIM, 4 * HDIM), 1) == target).astype(F32).astype(BF16)
    for h in range(HEADS):
        pieces = jnp.concatenate(
            [mine[2 * h], other[2 * h], mine[2 * h + 1], other[2 * h + 1]], axis=1
        )
        sorted_ = dot(pieces, pick).astype(BF16)
        proj[h, 0:128, :] = sorted_[:, : 3 * HDIM]
        for s in range(3):
            proj[h, 128:160, s * HDIM : (s + 1) * HDIM] = sorted_[
                s * PART : (s + 1) * PART, 3 * HDIM :
            ]
        proj[h, 160:256, :] = jnp.zeros((96, 3 * HDIM), BF16)

    query = iota((SPAN, SPAN), 0)
    key = iota((SPAN, SPAN), 1)
    back = jnp.concatenate([jnp.full((GROUP, SPAN), reach[j], jnp.int32) for j in range(FRAMES)], axis=0)
    allowed = (
        (query % GROUP == key % GROUP)
        & (key // GROUP <= query // GROUP)
        & (key // GROUP >= query // GROUP - back)
    )
    mask = jnp.where(allowed, F32(0.0), F32(-1e30))

    lane = iota((SPAN, HDIM), 1).astype(F32)
    sel_row = iota((HDIM, HDIM), 0)

    def level_at(step):
        sel = (sel_row == 96 + step).astype(F32).astype(BF16)
        rows = dot(received[:, 0:16, :].reshape(FRAMES * 16, HDIM), sel)
        return rows.reshape(FRAMES, 16, HDIM)[:, :GROUP].reshape(SPAN, HDIM)

    def groups(block):
        block = block.astype(F32)
        return [
            block[:, g * GROUP : (g + 1) * GROUP].reshape(SPAN, C) for g in range(POS // GROUP)
        ]

    def predict(tokens, level):
        hot = ((lane == level) | (lane == level + 32.0)).astype(F32).astype(BF16)
        full = jnp.concatenate(
            [
                jnp.concatenate([t.astype(BF16) for t in tokens], axis=0),
                jnp.concatenate([hot] * len(tokens), axis=0),
            ],
            axis=1,
        )
        hidden = dot(full, embed_in[...])
        scale = lax.rsqrt(jnp.mean(hidden * hidden, axis=-1, keepdims=True) + 1e-06)
        normed = (hidden * scale * gain[...]).astype(BF16)
        ones = jnp.ones((SPAN, HDIM), BF16)
        for h in range(HEADS):
            qkv = dot(full, proj[h]) * scale
            query = (qkv[:, :HDIM] * F32(math.log2(math.e) / math.sqrt(HDIM))).astype(BF16)
            keys = qkv[:, HDIM : 2 * HDIM].astype(BF16)
            values = qkv[:, 2 * HDIM :].astype(BF16)
            for g in range(len(tokens)):
                rows = slice(g * SPAN, (g + 1) * SPAN)
                scores = mask + lax.dot_general(
                    query[rows], keys[rows], (((1,), (1,)), ((), ())), preferred_element_type=F32
                )
                expo = jnp.exp2(scores - jnp.max(scores, axis=-1, keepdims=True)).astype(BF16)
                total = dot(expo, jnp.concatenate([values[rows], ones], axis=1))
                attn[rows, h * HDIM : (h + 1) * HDIM] = (
                    total[:, :HDIM] / total[:, HDIM:]
                ).astype(BF16)
        pred = dot(normed, w_res[...]) + dot(attn[...], w_out[...])
        return [pred[g * SPAN : (g + 1) * SPAN] for g in range(len(tokens))]

    first, second = level_at(0), level_at(1)
    share = [0.8 * sigma_of(l + 1.0) - sigma_of(l) for l in (first, second)]
    sigma = sigma_of(second)
    norm = jnp.sqrt(1.0 + sigma * sigma)
    preds = predict(groups(received[:, 32:48, :]), first)
    moved = [share[0] * p for p in preds]
    entering = fresh[pl.ds(pl.multiple_of(place[0] * POS, POS), POS), :]
    tokens = []
    for g, base in enumerate(groups(received[:, 48:64, :])):
        state = jnp.concatenate(
            [(base + moved[g])[GROUP:], entering[g * GROUP : (g + 1) * GROUP]], axis=0
        )
        tokens.append(state / norm)
    preds = predict(tokens, second)
    for g in range(POS // GROUP):
        kept = jnp.concatenate([moved[g][GROUP:], jnp.zeros((GROUP, C), F32)], axis=0)
        preds[g] = (kept + share[1] * preds[g]).reshape(FRAMES, 1, GROUP, C)
    out[...] = jnp.concatenate(preds, axis=1).reshape(FRAMES, POS, C).astype(BF16)


def shifted(block, axis, distance):
    devices = range(lax.axis_size(axis))
    route = [(i - distance, i) for i in devices if i - distance in devices]
    return lax.ppermute(block, axis, route)


def struct(shape, dtype):
    return jax.ShapeDtypeStruct(shape, dtype)


LIMIT = pltpu.CompilerParams(vmem_limit_bytes=40 * 1024 * 1024)


def on_device(window, noise, fresh, levels, reach, w_in, w_level, norm_gain, w_qkv, w_out, w_res):
    place = lax.axis_index("frame")
    gain = norm_gain.reshape(1, D)
    payload, base, late = pl.pallas_call(
        pack_kernel,
        out_shape=(
            struct((FRAMES, 64, C), BF16),
            struct((ROWS, C), F32),
            struct((ROWS, C), F32),
        ),
        in_specs=[SMEM, VMEM, VMEM, VMEM],
        out_specs=(VMEM, VMEM, VMEM),
        compiler_params=LIMIT,
        name="pack",
    )(levels, window, noise.reshape(2 * ROWS, C), w_qkv)
    received = lax.all_to_all(payload, "frame", split_axis=0, concat_axis=0, tiled=True)
    high, low, embed_in = pl.pallas_call(
        table_kernel,
        out_shape=(struct((160, D), BF16), struct((160, D), BF16), struct((256, D), BF16)),
        in_specs=[VMEM] * 4,
        out_specs=(VMEM,) * 3,
        compiler_params=LIMIT,
        name="tables",
    )(feats_table(), w_level, w_in, gain)
    packed = pl.pallas_call(
        project_kernel,
        out_shape=struct((FRAMES // 2, C, HDIM), BF16),
        in_specs=[VMEM] * 3,
        out_specs=VMEM,
        compiler_params=LIMIT,
        name="project",
    )(received, high, low)
    same_core = [list(range(core, FRAMES, 2)) for core in range(2)]
    mine = lax.all_to_all(
        packed, "frame", split_axis=0, concat_axis=0, tiled=True, axis_index_groups=same_core
    )
    other = lax.ppermute(mine, "frame", [(i, i ^ 1) for i in range(FRAMES)])
    delta = pl.pallas_call(
        passes_kernel,
        out_shape=struct((FRAMES, POS, C), BF16),
        in_specs=[SMEM, SMEM] + [VMEM] * 8,
        out_specs=VMEM,
        scratch_shapes=[
            pltpu.VMEM((HEADS, 256, 3 * HDIM), BF16),
            pltpu.VMEM((ROWS, HEADS * HDIM), BF16),
        ],
        compiler_params=LIMIT,
        name="passes",
    )(place.reshape(1), reach, received, mine, other, embed_in, gain, w_out, w_res, fresh)
    back = lax.all_to_all(delta, "frame", split_axis=0, concat_axis=0, tiled=True)
    moved = shifted(base, "frame", -1)
    start = jnp.where(place == FRAMES - 1, fresh, moved)
    return start + late + back.reshape(ROWS, C).astype(F32)


def solution(mesh):
    return jax.shard_map(
        on_device,
        mesh=mesh,
        in_specs=(
            P(("batch", "frame"), None),
            P(("batch", "frame"), None, None),
            P("batch", None),
            P(("batch", "frame"), None),
            P("batch"),
            P(),
            P(),
            P(),
            P("frame", None),
            P(),
            P(),
        ),
        out_specs=P(("batch", "frame"), None),
        check_vma=False,
    )
```

time: 378 us -> 85.1 us (0.23)
  waiting for transfers between devices: 203 us -> 25.2 us
  blocking collectives: 78 us -> 18.7 us
  matrix products: 39.8 us -> 0 us
  local copies, waits for them, and re-layouts: 21.5 us -> 4.23 us
  between operations: 16.5 us -> 0.17 us
  Pallas kernels: 0 us -> 13.7 us
    all_to_all x3 -> x2, waiting for transfers between devices: 123 us -> 25.2 us  [the longest x1 16.5 us: on_device(): lax.all_to_all(payload, 'frame', split_axis=0, concat_axis=0, tiled=True)]
    all_gather x1 -> x0, waiting for transfers between devices: 73.7 us -> none  [on_device(): full_weights = lax.all_gather(w_qkv, 'frame', axis=0, tiled=True)]
    all_to_all x1, blocking collectives: 78 us -> 18.7 us  [on_device(): lax.all_to_all(packed, 'frame', split_axis=0, concat_axis=0, tiled=True,...]
    dot_general x12 -> x0, matrix products: 30.3 us -> none  [the longest x2 14.3 us: on_device(): jnp.dot(normed, full_weights, preferred_element_type=jnp.float32)]
    pallas_call x0 -> x4, Pallas kernels: none -> 13.7 us  [the longest x1 11.3 us: on_device(): pl.pallas_call(passes_kernel, out_shape=struct((FRAMES, POS, C), BF16), i...]
    sub x2 -> x0, matrix products: 9.58 us -> none  [attention(): expo = jnp.exp(scores - top)]
    slice x4 -> x0, local copies, waits for them, and re-layouts: 6.46 us -> none  [the longest x2 2.65 us: attention(): values = block[:, :, 2 * width:].reshape(frames, count, HEADS, HDIM)]
    ppermute x1, waiting for transfers between devices: 5.39 us -> 0.01 us  [shifted(): return lax.ppermute(block, axis, route)]
  transfers between devices with their start and end apart: 5 -> 4, of which waited for: 5 -> 2; matrix products, arithmetic and copies ran while one was open for 2% -> 0% of each run, Pallas kernels for 0% -> 14%
where the time goes in v1:
time: 85.1 us; the launch traced here: 84.7 us
  waiting for transfers between devices  25.2 us (30%)
  starting transfers between devices  20.9 us (25%)
  blocking collectives  18.7 us (22%)
  Pallas kernels  13.7 us (16%)
  local copies, waits for them, and re-layouts  4.23 us (5%)
  other arithmetic  1.7 us (2%)
    all_to_all x1, blocking collectives, on_device(): lax.all_to_all(packed, 'frame', split_axis=0, concat_axis=0, tiled=True,...  18.7 us
    all_to_all x1, waiting for transfers between devices, on_device(): lax.all_to_all(payload, 'frame', split_axis=0, concat_axis=0, tiled=True)  16.5 us
    all_to_all x1, starting transfers between devices, on_device(): lax.all_to_all(payload, 'frame', split_axis=0, concat_axis=0, tiled=True)  11.5 us
    pallas_call x1, Pallas kernels, on_device(): pl.pallas_call(passes_kernel, out_shape=struct((FRAMES, POS, C), BF16), i...  11.3 us
    all_to_all x1, waiting for transfers between devices, on_device(): lax.all_to_all(delta, 'frame', split_axis=0, concat_axis=0, tiled=True)  8.7 us
    unnamed x24, local copies, waits for them, and re-layouts  4.23 us
    all_to_all x1, starting transfers between devices, on_device(): lax.all_to_all(delta, 'frame', split_axis=0, concat_axis=0, tiled=True)  3.89 us
    ppermute x1, starting transfers between devices, on_device(): other = lax.ppermute(mine, 'frame', [(i, i ^ 1) for i in range(FRAMES)])  3.59 us
  transfers between devices with their start and end apart: 4, of which 2 were waited for; matrix products, arithmetic and copies ran while one was open for 0% of the time, Pallas kernels for 14%

profile of v1, /device:TPU:1, one launch (start us, length us, event | category | flops | bytes accessed | tf_op | source)
XLA Modules:
  0.0 84.7 jit_solution(11028860472350746693)
XLA Ops:
  0.0 0.7 copy-done.10
  0.7 1.0 %copy-done.1 = f32[512,2,128]{2,1,0:T(2,128)S(1)} copy-done((f32[512,2,128]{2,1,0:T(2,128)S(1)}, f32[512,2,128]{2,1,0:T(2,128)}, u32[]{:S(2)}) %copy-start.1) | copy-done | bytes 524312
  1.7 0.9 %copy-done.3 = f32[512,128]{1,0:T(8,128)S(1)} copy-done((f32[512,128]{1,0:T(8,128)S(1)}, f32[512,128]{1,0:T(8,128)}, u32[]{:S(2)}) %copy-start.3) | copy-done | bytes 262168
  2.7 0.9 %copy-done.7 = bf16[32,3072]{1,0:T(8,128)(2,1)S(1)} copy-done((bf16[32,3072]{1,0:T(8,128)(2,1)S(1)}, bf16[32,3072]{1,0:T(8,128)(2,1)}, u32[]{:S(2)}) %copy-start.7) | copy-done | bytes 196632
  3.6 1.7 %pack.1 = (bf16[32,64,128]{2,1,0:T(8,128)(2,1)}, f32[512,128]{1,0:T(8,128)S(1)}, f32[512,128]{1,0:T(8,128)S(1)}) custom-call(s32[1,2]{1,0:T(1,128)S(1)} %copy-done.10, f32[512,128]{1,0:T(8,128)S(1)} %copy-done.3, f32[1024,128]{1,0:T(8,128)S(1)} %bitcast.6, bf16[32,3072]{1,0:T(8,128)(2,1)S(1)} %copy-done.7), custom_call_target="tpu_custom_call" | custom-call | tf_op jit(solution)/shard_map/pack/pallas_call | solution.py:217
  5.3 11.5 %all-to-all-start = ((bf16[32,64,128]{2,1,0:T(8,128)(2,1)}), bf16[32,64,128]{2,1,0:T(8,128)(2,1)S(1)}, u32[]{:S(2)}, u32[]{:S(2)}) async-start(bf16[32,64,128]{2,1,0:T(8,128)(2,1)} %get-tuple-element.13), calls=%async_computation | async-start | bytes 1048576 | tf_op jit(solution)/shard_map/all_to_all | solution.py:229
  16.9 0.3 tables.1
  17.2 16.5 %all-to-all-done.received = bf16[32,64,128]{2,1,0:T(8,128)(2,1)S(1)} async-done(((bf16[32,64,128]{2,1,0:T(8,128)(2,1)}), bf16[32,64,128]{2,1,0:T(8,128)(2,1)S(1)}, u32[]{:S(2)}, u32[]{:S(2)}) %all-to-all-start) | async-done | bytes 524320 | tf_op jit(solution)/shard_map/all_to_all | solution.py:229
  33.7 0.4 project.1
  34.1 0.0 copy-start
  34.1 0.0 copy-start.5
  34.1 0.0 copy-start.6
  34.1 18.7 %all_to_all.15.mine = bf16[16,128,128]{2,1,0:T(8,128)(2,1)S(1)} all-to-all(bf16[16,128,128]{2,1,0:T(8,128)(2,1)S(1)} %project.1), channel_id=1, replica_groups={{0,32,64,96,128,160,192,224,256,288,320,352,384,416,448,480},{16,48,80,..., dimensions={0} | all-to-all | bytes 1048576 | tf_op jit(solution)/shard_map/all_to_all | solution.py:247
  52.9 3.6 %collective-permute-start.1 = (bf16[16,128,128]{2,1,0:T(8,128)(2,1)S(1)}, bf16[16,128,128]{2,1,0:T(8,128)(2,1)S(1)}, u32[]{:S(2)}, u32[]{:S(2)}) collective-permute-start(bf16[16,128,128]{2,1,0:T(8,128)(2,1)S(1)} %all_to_all.15.mine), channel_id=1, source_target_pairs={{0,16},{16,0},{32,48},{48,32},{64,80},{80,64},{96,112},{112,96},{1... | collective-permute-start | bytes 1572872 | tf_op jit(solution)/shard_map/ppermute | solution.py:250
  56.5 1.9 %collective-permute-start = (f32[512,128]{1,0:T(8,128)S(1)}, f32[512,128]{1,0:T(8,128)}, u32[]{:S(2)}, u32[]{:S(2)}) collective-permute-start(f32[512,128]{1,0:T(8,128)S(1)} %get-tuple-element.11), channel_id=1, source_target_pairs={{16,0},{32,16},{48,32},{64,48},{80,64},{96,80},{112,96},{128,112},... | collective-permute-start | bytes 786440 | tf_op jit(solution)/shard_map/ppermute | solution.py:204
  58.4 0.0 collective-permute-done.1.other
  58.4 0.0 copy-start.11
  58.4 0.0 copy-done
  58.4 0.6 copy-done.11
  59.1 11.3 %passes.1 = bf16[32,16,128]{2,1,0:T(8,128)(2,1)} custom-call(s32[1]{0:T(128)} %bitcast.1.place, s32[32]{0:T(128)S(1)} %copy-done.11, bf16[32,64,128]{2,1,0:T(8,128)(2,1)S(1)} %all-to-all-done.received, bf16[16,128,128]{2,1,0:T(8,128)(2,1)S(1)} %all_to_all.15.mine, bf16[16,128,128]{2,1,0:T(8,128)(2,1)S(1)} %collective-permute-done.1.other, ...), custom_call_target="tpu_custom_call" | custom-call | tf_op jit(solution)/shard_map/passes/pallas_call | solution.py:251
  70.3 3.9 %all-to-all-start.2 = ((bf16[32,16,128]{2,1,0:T(8,128)(2,1)}), bf16[32,16,128]{2,1,0:T(8,128)(2,1)S(1)}, u32[]{:S(2)}, u32[]{:S(2)}) async-start(bf16[32,16,128]{2,1,0:T(8,128)(2,1)} %passes.1), calls=%async_computation.2 | async-start | bytes 262144 | tf_op jit(solution)/shard_map/all_to_all | solution.py:263
  74.2 0.0 collective-permute-done
  74.3 8.7 %all-to-all-done.2 = bf16[32,16,128]{2,1,0:T(8,128)(2,1)S(1)} async-done(((bf16[32,16,128]{2,1,0:T(8,128)(2,1)}), bf16[32,16,128]{2,1,0:T(8,128)(2,1)S(1)}, u32[]{:S(2)}, u32[]{:S(2)}) %all-to-all-start.2) | async-done | bytes 131104 | tf_op jit(solution)/shard_map/all_to_all | solution.py:263
  83.0 1.7 %convert_add_fusion = f32[512,128]{1,0:T(8,128)} fusion(f32[512,128]{1,0:T(8,128)S(1)} %get-tuple-element.12, f32[512,128]{1,0:T(8,128)S(1)} %copy-done, f32[512,128]{1,0:T(8,128)} %collective-permute-done, bf16[32,16,128]{2,1,0:T(8,128)(2,1)S(1)} %all-to-all-done.2, pred[]{:T(512)S(6)} %eq.3), kind=kLoop, calls=%fused_computation | loop fusion | flops 262144 | bytes 1179649 | tf_op jit(solution)/shard_map/add | solution.py:266
  (14 shorter events, 0.0 us)
Async XLA Ops:
  0.0 0.7 copy-start.10
  0.7 1.0 %copy-start.1 = (f32[512,2,128]{2,1,0:T(2,128)S(1)}, f32[512,2,128]{2,1,0:T(2,128)}, u32[]{:S(2)}) copy-start(f32[512,2,128]{2,1,0:T(2,128)} %param.13) | copy-start | bytes 1572868
  1.7 0.9 %copy-start.3 = (f32[512,128]{1,0:T(8,128)S(1)}, f32[512,128]{1,0:T(8,128)}, u32[]{:S(2)}) copy-start(f32[512,128]{1,0:T(8,128)} %window.1) | copy-start | bytes 786436
  2.6 0.9 %copy-start.7 = (bf16[32,3072]{1,0:T(8,128)(2,1)S(1)}, bf16[32,3072]{1,0:T(8,128)(2,1)}, u32[]{:S(2)}) copy-start(bf16[32,3072]{1,0:T(8,128)(2,1)} %w_qkv.1) | copy-start | bytes 589828
  5.3 11.5 %copy-start.2 = (bf16[256,1024]{1,0:T(8,128)(2,1)S(1)}, bf16[256,1024]{1,0:T(8,128)(2,1)}, u32[]{:S(2)}) copy-start(bf16[256,1024]{1,0:T(8,128)(2,1)} %w_level.1) | copy-start | bytes 1572868
  5.3 11.6 %copy-start.4 = (bf16[128,1024]{1,0:T(8,128)(2,1)S(1)}, bf16[128,1024]{1,0:T(8,128)(2,1)}, u32[]{:S(2)}) copy-start(bf16[128,1024]{1,0:T(8,128)(2,1)} %w_in.1) | copy-start | bytes 786436
  5.3 11.6 %copy-start.8 = (f32[1024]{0:T(1024)S(1)}, f32[1024]{0:T(1024)}, u32[]{:S(2)}) copy-start(f32[1024]{0:T(1024)} %param.19) | copy-start | bytes 12292
  5.3 11.6 %copy-start.9 = (bf16[32,256]{1,0:T(8,128)(2,1)S(1)}, bf16[32,256]{1,0:T(8,128)(2,1)}, u32[]{:S(2)}) copy-start(bf16[32,256]{1,0:T(8,128)(2,1)} %constant.12.feats) | copy-start | bytes 49156
  5.3 28.3 %all-to-all-start = ((bf16[32,64,128]{2,1,0:T(8,128)(2,1)}), bf16[32,64,128]{2,1,0:T(8,128)(2,1)S(1)}, u32[]{:S(2)}, u32[]{:S(2)}) async-start(bf16[32,64,128]{2,1,0:T(8,128)(2,1)} %get-tuple-element.13), calls=%async_computation | async-start | bytes 1048576 | tf_op jit(solution)/shard_map/all_to_all | solution.py:229
  34.1 24.3 %copy-start = (f32[512,128]{1,0:T(8,128)S(1)}, f32[512,128]{1,0:T(8,128)}, u32[]{:S(2)}) copy-start(f32[512,128]{1,0:T(8,128)} %fresh.1) | copy-start | bytes 786436
  34.1 24.3 %copy-start.5 = (bf16[1024,128]{1,0:T(8,128)(2,1)S(1)}, bf16[1024,128]{1,0:T(8,128)(2,1)}, u32[]{:S(2)}) copy-start(bf16[1024,128]{1,0:T(8,128)(2,1)} %w_out.1) | copy-start | bytes 786436
  34.1 24.3 %copy-start.6 = (bf16[1024,128]{1,0:T(8,128)(2,1)S(1)}, bf16[1024,128]{1,0:T(8,128)(2,1)}, u32[]{:S(2)}) copy-start(bf16[1024,128]{1,0:T(8,128)(2,1)} %w_res.1) | copy-start | bytes 786436
  52.9 5.5 %collective-permute-start.1 = (bf16[16,128,128]{2,1,0:T(8,128)(2,1)S(1)}, bf16[16,128,128]{2,1,0:T(8,128)(2,1)S(1)}, u32[]{:S(2)}, u32[]{:S(2)}) collective-permute-start(bf16[16,128,128]{2,1,0:T(8,128)(2,1)S(1)} %all_to_all.15.mine), channel_id=1, source_target_pairs={{0,16},{16,0},{32,48},{48,32},{64,80},{80,64},{96,112},{112,96},{1... | collective-permute-start | bytes 1572872 | tf_op jit(solution)/shard_map/ppermute | solution.py:250
  56.5 17.8 %collective-permute-start = (f32[512,128]{1,0:T(8,128)S(1)}, f32[512,128]{1,0:T(8,128)}, u32[]{:S(2)}, u32[]{:S(2)}) collective-permute-start(f32[512,128]{1,0:T(8,128)S(1)} %get-tuple-element.11), channel_id=1, source_target_pairs={{16,0},{32,16},{48,32},{64,48},{80,64},{96,80},{112,96},{128,112},... | collective-permute-start | bytes 786440 | tf_op jit(solution)/shard_map/ppermute | solution.py:204
  58.4 0.7 copy-start.11
  70.3 12.6 %all-to-all-start.2 = ((bf16[32,16,128]{2,1,0:T(8,128)(2,1)}), bf16[32,16,128]{2,1,0:T(8,128)(2,1)S(1)}, u32[]{:S(2)}, u32[]{:S(2)}) async-start(bf16[32,16,128]{2,1,0:T(8,128)(2,1)} %passes.1), calls=%async_computation.2 | async-start | bytes 262144 | tf_op jit(solution)/shard_map/all_to_all | solution.py:263

commit v2 on v1

v2 whole, which is shorter than its diff:
```python
import math

import jax
import jax.numpy as jnp
import numpy as np
from jax import lax
from jax.experimental import pallas as pl
from jax.experimental.pallas import tpu as pltpu
from jax.sharding import PartitionSpec as P

HEADS = 8
HDIM = 128
C = 128
D = 1024
FREQ = 128
LEVELS = 32
FRAMES = 32
ROWS = 512
POS = ROWS // FRAMES
GROUP = 8
SPAN = FRAMES * GROUP
PART = 32
DECAY = math.log(1.0 / 16.0) / LEVELS
BF16 = jnp.bfloat16
F32 = jnp.float32
VMEM = pl.BlockSpec(memory_space=pltpu.VMEM)
SMEM = pl.BlockSpec(memory_space=pltpu.SMEM)
HBM = pl.BlockSpec(memory_space=pltpu.HBM)


def sigma_of(level):
    return 4.0 * jnp.exp(level * F32(DECAY))


def feats_table():
    sigma = 4.0 * np.exp(np.arange(LEVELS) * DECAY)
    freqs = np.exp(np.arange(FREQ) * (math.log(100.0) / FREQ))
    angle = np.log(sigma)[:, None] * freqs[None, :]
    return jnp.asarray(np.concatenate([np.sin(angle), np.cos(angle)], axis=1), F32).astype(BF16)


def dot(a, b):
    return jnp.dot(a, b, preferred_element_type=F32)


def iota(shape, dim):
    return lax.broadcasted_iota(jnp.int32, shape, dim)


def pack_kernel(levels, window_in, noise_in, w_qkv_in, out, base_out, window, noise, w_qkv, sems):
    copies = [
        pltpu.make_async_copy(src, dst, sems.at[k])
        for k, (src, dst) in enumerate(
            [(w_qkv_in, w_qkv), (window_in, window), (noise_in, noise)]
        )
    ]
    for copy in copies:
        copy.start()
    first = jnp.full((8, C), levels[0, 0], jnp.int32).astype(F32)
    second = jnp.full((8, C), levels[0, 1], jnp.int32).astype(F32)
    row = iota((3 * HDIM, 1), 0)
    target = (row % HDIM) // PART * HDIM + row // HDIM * PART + row % PART
    pick = (iota((3 * HDIM, 4 * HDIM), 1) == target).astype(F32).astype(BF16)
    lane = iota((PART, HDIM), 1)
    sigma = sigma_of(first)[:1]
    odd = lax.axis_index("batch") % 2
    copies[0].wait()
    stacked = jnp.concatenate(
        [
            jnp.concatenate(
                [
                    w_qkv[:, pl.ds(pl.multiple_of((s * HEADS + 2 * x + odd) * HDIM, HDIM), HDIM)]
                    for s in range(3)
                ],
                axis=1,
            )
            for x in range(4)
        ],
        axis=0,
    )
    pieces = dot(stacked, pick)
    for x in range(4):
        for i in range(4):
            piece = pieces[x * PART : (x + 1) * PART, i * HDIM : (i + 1) * HDIM]
            piece = jnp.where(lane == 96, first[:1], jnp.where(lane == 97, second[:1], piece))
            piece = piece.astype(BF16)
            out[x * 8 + i, 0:32, :] = piece
            out[x * 8 + i + 4, 0:32, :] = piece
    copies[1].wait()
    state = window[...]
    scaled = state / jnp.sqrt(1.0 + sigma * sigma)
    out[:, 32:48, :] = scaled.reshape(FRAMES, POS, C).astype(BF16)
    copies[2].wait()
    base = state + (0.6 * sigma_of(first + 1.0)[:1]) * noise[pl.ds(0, ROWS, stride=2), :]
    base_out[...] = base
    out[:, 48:64, :] = base.reshape(FRAMES, POS, C).astype(BF16)


def split(value):
    high = value.astype(BF16)
    return high, (value - high.astype(F32)).astype(BF16)


def table_kernel(feats, w_level, w_in, gain, w_res, high, low, embed_in, residual):
    emb = dot(feats[...], w_level[...])
    embed_in[0:128, :] = w_in[...]
    embed_in[128:160, :], embed_in[160:192, :] = split(emb)
    embed_in[192:256, :] = jnp.zeros((64, D), BF16)
    scaled = jnp.concatenate([w_in[...].astype(F32), emb], axis=0) * gain[...]
    high[...], low[...] = split(scaled)
    residual[...] = jnp.zeros((512, C), BF16)
    product = dot(high[...], w_res[...]) + dot(low[...], w_res[...])
    residual[0:160, :], residual[256:416, :] = split(product)


def project_kernel(received, high, low, out):
    part = received[:, 0:32, :].reshape(D, HDIM)
    lane = iota((C, HDIM), 1)
    product = dot(high[...], part) + dot(low[...], part)
    product *= jnp.where(lane[:1] < PART, F32(math.log2(math.e) / math.sqrt(HDIM)), F32(1.0))
    emb = product[128:160]
    beside = jnp.concatenate(
        [pltpu.roll(emb, 96, 1), pltpu.roll(emb, 64, 1), pltpu.roll(emb, 32, 1), jnp.zeros_like(emb)],
        axis=0,
    )
    packed = jnp.where(lane < 96, product[:128], beside).astype(BF16)
    out[...] = jnp.broadcast_to(packed[None], out.shape)


def normalised(tokens, hot, embed_in, residual):
    full = jnp.concatenate([tokens.astype(BF16), hot], axis=1)
    hidden = dot(full, embed_in[...])
    scale = lax.rsqrt(jnp.mean(hidden * hidden, axis=-1, keepdims=True) + 1e-06)
    scale = jnp.broadcast_to(scale, (ROWS, C))
    kept = scale * (dot(full, residual[0:256, :]) + dot(full, residual[256:512, :]))
    halves = [(full[:, k * C : (k + 1) * C].astype(F32) * scale).astype(BF16) for k in range(2)]
    return jnp.concatenate(halves, axis=1), kept


def groups_of(block):
    block = block.astype(F32)
    return jnp.concatenate(
        [block[:, g * GROUP : (g + 1) * GROUP].reshape(SPAN, C) for g in range(POS // GROUP)],
        axis=0,
    )


def before_kernel(
    levels, reach, received, embed_in, residual, fresh, moved, noise, w_out_in,
    normed, kept, base, hot, scales, mask, entering, w_out, start,
):
    place = lax.axis_index("frame")
    last = jnp.full((8, C), place, jnp.int32)[:1] == FRAMES - 1
    level = jnp.full((8, C), levels[0, 1], jnp.int32).astype(F32)[:1]
    late = (0.6 * sigma_of(level + 1.0)) * noise[pl.ds(1, ROWS, stride=2), :]
    start[...] = jnp.where(last, fresh[...], moved[...]) + late
    w_out[...] = w_out_in[...]
    entering[...] = fresh[pl.ds(pl.multiple_of(place * POS, POS), POS), :]
    query = iota((SPAN, SPAN), 0)
    key = iota((SPAN, SPAN), 1)
    back = jnp.concatenate([jnp.full((GROUP, SPAN), reach[j], jnp.int32) for j in range(FRAMES)], axis=0)
    allowed = (
        (query % GROUP == key % GROUP)
        & (key // GROUP <= query // GROUP)
        & (key // GROUP >= query // GROUP - back)
    )
    mask[...] = jnp.where(allowed, F32(0.0), F32(-1e30))
    lane = iota((SPAN, HDIM), 1).astype(F32)
    sel_row = iota((HDIM, HDIM), 0)
    hots = []
    for step in range(2):
        sel = (sel_row == 96 + step).astype(F32).astype(BF16)
        rows = dot(received[:, 0:16, :].reshape(FRAMES * 16, HDIM), sel)
        level = rows.reshape(FRAMES, 16, HDIM)[:, :GROUP].reshape(SPAN, HDIM)
        sigma = sigma_of(level)
        scales[step] = 0.8 * sigma_of(level + 1.0) - sigma
        if step:
            scales[2] = 1.0 / jnp.sqrt(1.0 + sigma * sigma)
        hots.append(((lane == level) | (lane == level + 32.0)).astype(F32).astype(BF16))
    hot[...] = hots[1]
    tokens = groups_of(received[:, 32:48, :])
    base[...] = groups_of(received[:, 48:64, :])
    normed[...], kept[...] = normalised(
        tokens, jnp.concatenate([hots[0], hots[0]], axis=0), embed_in, residual
    )


def passes_kernel(
    mine, other, embed_in, residual, normed, kept, base, hot, scales, mask, entering, w_out,
    out, pairs, values, attn,
):
    core = lax.axis_index("frame") % 2
    row = iota((4 * HDIM, 1), 0)
    piece = row // HDIM
    target = row % HDIM // PART * HDIM + (piece + core - 2 * (piece % 2) * core) * PART + row % PART
    pick = (iota((4 * HDIM, 4 * HDIM), 1) == target).astype(F32).astype(BF16)
    for h in range(HEADS):
        pieces = jnp.concatenate(
            [mine[2 * h], other[2 * h], mine[2 * h + 1], other[2 * h + 1]], axis=1
        )
        ordered = dot(pieces, pick).astype(BF16)
        beside = slice(h % 2 * HDIM, (h % 2 + 1) * HDIM)
        pairs[h, 0:128, :] = ordered[:, : 2 * HDIM]
        values[h // 2, 0:128, beside] = ordered[:, 2 * HDIM : 3 * HDIM]
        pairs[h, 128:160, :HDIM] = ordered[0:32, 3 * HDIM :]
        pairs[h, 128:160, HDIM:] = ordered[32:64, 3 * HDIM :]
        values[h // 2, 128:160, beside] = ordered[64:96, 3 * HDIM :]
        pairs[h, 160:256, :] = jnp.zeros((96, 2 * HDIM), BF16)
        values[h // 2, 160:256, beside] = jnp.zeros((96, HDIM), BF16)
    ones = jnp.ones((SPAN, HDIM), BF16)

    def predict(normed, kept):
        for h in range(HEADS):
            query_key = dot(normed, pairs[h]).astype(BF16)
            if h % 2 == 0:
                both = dot(normed, values[h // 2]).astype(BF16)
            for g in range(POS // GROUP):
                rows = slice(g * SPAN, (g + 1) * SPAN)
                scores = mask[...] + lax.dot_general(
                    query_key[rows, :HDIM],
                    query_key[rows, HDIM:],
                    (((1,), (1,)), ((), ())),
                    preferred_element_type=F32,
                )
                expo = jnp.exp2(scores - jnp.max(scores, axis=-1, keepdims=True)).astype(BF16)
                value = both[rows, h % 2 * HDIM : (h % 2 + 1) * HDIM]
                total = dot(expo, jnp.concatenate([value, ones], axis=1))
                attn[rows, h * HDIM : (h + 1) * HDIM] = (
                    total[:, :HDIM] / total[:, HDIM:]
                ).astype(BF16)
        return kept + dot(attn[...], w_out[...])

    def both_groups(block):
        return jnp.concatenate([block] * (POS // GROUP), axis=0)

    def next_slot(block, entering):
        parts = []
        for g in range(POS // GROUP):
            parts += [block[g * SPAN + GROUP : (g + 1) * SPAN], entering[g * GROUP : (g + 1) * GROUP]]
        return jnp.concatenate(parts, axis=0)

    moved = both_groups(scales[0]) * predict(normed[...], kept[...])
    tokens = next_slot(base[...] + moved, entering[...]) * both_groups(scales[2])
    delta = both_groups(scales[1]) * predict(
        *normalised(tokens, both_groups(hot[...]), embed_in, residual)
    )
    delta += next_slot(moved, jnp.zeros((POS, C), F32))
    parts = [
        delta[g * SPAN : (g + 1) * SPAN].reshape(FRAMES, 1, GROUP, C) for g in range(POS // GROUP)
    ]
    out[...] = jnp.concatenate(parts, axis=1).reshape(FRAMES, POS, C).astype(BF16)


def shifted(block, axis, distance):
    devices = range(lax.axis_size(axis))
    route = [(i - distance, i) for i in devices if i - distance in devices]
    return lax.ppermute(block, axis, route)


def struct(shape, dtype):
    return jax.ShapeDtypeStruct(shape, dtype)


LIMIT = 40 * 1024 * 1024


def spread_groups(batches):
    across = min(batches, 8)
    deep = batches // across * 4

    def index(x, y, z, core):
        return (x * 8 + z % 4 * 2 + core) * batches + z // 4 * across + y

    def pairs(length):
        return [(k, k + 1) for k in range(0, length, 2)]

    return [
        [index(x, y, z, core) for x in range(4) for y in ys for z in zs]
        for core in range(2)
        for ys in pairs(across)
        for zs in pairs(deep)
    ]


def call(kernel, name, out_shape, in_specs, cost, scratch_shapes=(), limit=LIMIT):
    flops, bytes_accessed = cost
    return pl.pallas_call(
        kernel,
        out_shape=out_shape,
        in_specs=in_specs,
        out_specs=jax.tree.map(lambda _: VMEM, out_shape),
        scratch_shapes=scratch_shapes,
        compiler_params=pltpu.CompilerParams(vmem_limit_bytes=limit),
        cost_estimate=pl.CostEstimate(
            flops=flops, bytes_accessed=bytes_accessed, transcendentals=0
        ),
        name=name,
    )


def on_device(window, noise, fresh, levels, reach, w_in, w_level, norm_gain, w_qkv, w_out, w_res):
    pairs_of_noise = noise.reshape(2 * ROWS, C)
    payload, base = call(
        pack_kernel,
        "pack",
        (struct((FRAMES, 64, C), BF16), struct((ROWS, C), F32)),
        [SMEM] + [HBM] * 3,
        (10**8, 2 * 10**6),
        [
            pltpu.VMEM((ROWS, C), F32),
            pltpu.VMEM((2 * ROWS, C), F32),
            pltpu.VMEM((D // FRAMES, 3 * D), BF16),
            pltpu.SemaphoreType.DMA((3,)),
        ],
        None,
    )(levels, window, pairs_of_noise, w_qkv)
    received = lax.all_to_all(payload, "frame", split_axis=0, concat_axis=0, tiled=True)
    moved = shifted(base, "frame", -1)
    moved, w_level = lax.optimization_barrier((moved, w_level))
    high, low, embed_in, residual = call(
        table_kernel,
        "tables",
        (
            struct((160, D), BF16),
            struct((160, D), BF16),
            struct((256, D), BF16),
            struct((512, C), BF16),
        ),
        [VMEM] * 5,
        (10**8, 3 * 10**6),
    )(feats_table(), w_level, w_in, norm_gain.reshape(1, D), w_res)
    packed = call(
        project_kernel,
        "project",
        struct((FRAMES // 2, C, HDIM), BF16),
        [VMEM] * 3,
        (10**8, 2 * 10**6),
    )(received, high, low)
    mine = lax.all_to_all(
        packed,
        ("frame", "batch"),
        split_axis=0,
        concat_axis=0,
        tiled=True,
        axis_index_groups=spread_groups(lax.axis_size("batch")),
    )
    *prepared, start = call(
        before_kernel,
        "before",
        (
            struct((ROWS, 2 * C), BF16),
            struct((ROWS, C), F32),
            struct((ROWS, C), F32),
            struct((SPAN, C), BF16),
            struct((3, SPAN, C), F32),
            struct((SPAN, SPAN), F32),
            struct((POS, C), F32),
            struct((D, C), BF16),
            struct((ROWS, C), F32),
        ),
        [SMEM, SMEM] + [VMEM] * 7,
        (4 * 10**8, 4 * 10**6),
    )(levels, reach, received, embed_in, residual, fresh, moved, pairs_of_noise, w_out)
    other = lax.ppermute(mine, "frame", [(i, i ^ 1) for i in range(FRAMES)])
    delta = call(
        passes_kernel,
        "passes",
        struct((FRAMES, POS, C), BF16),
        [VMEM] * 12,
        (5 * 10**9, 4 * 10**6),
        [
            pltpu.VMEM((HEADS, 256, 2 * HDIM), BF16),
            pltpu.VMEM((HEADS // 2, 256, 2 * HDIM), BF16),
            pltpu.VMEM((ROWS, HEADS * HDIM), BF16),
        ],
    )(mine, other, embed_in, residual, *prepared)
    back = lax.all_to_all(delta, "frame", split_axis=0, concat_axis=0, tiled=True)
    return start + back.reshape(ROWS, C).astype(F32)


def solution(mesh):
    return jax.shard_map(
        on_device,
        mesh=mesh,
        in_specs=(
            P(("batch", "frame"), None),
            P(("batch", "frame"), None, None),
            P("batch", None),
            P(("batch", "frame"), None),
            P("batch"),
            P(),
            P(),
            P(),
            P("frame", None),
            P(),
            P(),
        ),
        out_specs=P(("batch", "frame"), None),
        check_vma=False,
    )
```

time: 85.1 us -> 74.2 us (0.87)
  waiting for transfers between devices: 25.2 us -> 14.1 us
  blocking collectives: 18.7 us -> 29.5 us
  starting transfers between devices: 20.9 us -> 15.6 us
  local copies, waits for them, and re-layouts: 4.23 us -> 0.68 us
  other arithmetic: 1.7 us -> 0.73 us
    all_to_all x1, waiting for transfers between devices: 16.5 us -> 3.21 us  [on_device(): lax.all_to_all(payload, 'frame', split_axis=0, concat_axis=0, tiled=True)]
    ppermute x1, waiting for transfers between devices: 0.01 us -> 10.9 us  [shifted(): return lax.ppermute(block, axis, route)]
    all_to_all x1 -> x2, blocking collectives: 18.7 us -> 29.5 us  [the longest x1 15.6 us: on_device(): lax.all_to_all(packed, ('frame', 'batch'), split_axis=0, concat_axis=0, t...]
    all_to_all x1 -> x0, waiting for transfers between devices: 8.7 us -> none  [on_device(): lax.all_to_all(delta, 'frame', split_axis=0, concat_axis=0, tiled=True)]
    all_to_all x1 -> x0, starting transfers between devices: 3.89 us -> none  [on_device(): lax.all_to_all(delta, 'frame', split_axis=0, concat_axis=0, tiled=True)]
    unnamed x24 -> x20, local copies, waits for them, and re-layouts: 4.23 us -> 0.68 us
    ppermute x1, starting transfers between devices: 3.59 us -> 1.91 us  [on_device(): other = lax.ppermute(mine, 'frame', [(i, i ^ 1) for i in range(FRAMES)])]
    add x1, other arithmetic: 1.7 us -> 0.73 us  [on_device(): return start + back.reshape(ROWS, C).astype(F32)]
  transfers between devices with their start and end apart: 4 -> 3, of which waited for: 2 -> 2; matrix products, arithmetic and copies ran while one was open for 0% -> 0% of each run, Pallas kernels for 14% -> 3%
where the time goes in v2:
time: 74.2 us; the launch traced here: 73.8 us
  blocking collectives  29.5 us (40%)
  starting transfers between devices  15.6 us (21%)
  waiting for transfers between devices  14.1 us (19%)
  Pallas kernels  13 us (18%)
    all_to_all x1, blocking collectives, on_device(): lax.all_to_all(packed, ('frame', 'batch'), split_axis=0, concat_axis=0, t...  15.6 us
    all_to_all x1, blocking collectives, on_device(): lax.all_to_all(delta, 'frame', split_axis=0, concat_axis=0, tiled=True)  13.9 us
    all_to_all x1, starting transfers between devices, on_device(): lax.all_to_all(payload, 'frame', split_axis=0, concat_axis=0, tiled=True)  11.5 us
    ppermute x1, waiting for transfers between devices, shifted(): return lax.ppermute(block, axis, route)  10.9 us
    pallas_call x1, Pallas kernels, on_device(): call(passes_kernel, 'passes', struct((FRAMES, POS, C), BF16), [VMEM] * 12...  7.56 us
    all_to_all x1, waiting for transfers between devices, on_device(): lax.all_to_all(payload, 'frame', split_axis=0, concat_axis=0, tiled=True)  3.21 us
    pallas_call x1, Pallas kernels, on_device(): call(pack_kernel, 'pack', (struct((FRAMES, 64, C), BF16), struct((ROWS, C...  2.96 us
    ppermute x1, starting transfers between devices, shifted(): return lax.ppermute(block, axis, route)  2.14 us
  transfers between devices with their start and end apart: 3, of which 2 were waited for; matrix products, arithmetic and copies ran while one was open for 0% of the time, Pallas kernels for 3%

profile of v2, /device:TPU:1, one launch (start us, length us, event | category | flops | bytes accessed | tf_op | source)
XLA Modules:
  0.0 73.8 jit_solution(4577091279287081707)
XLA Ops:
  0.0 3.0 %pack.1 = (bf16[32,64,128]{2,1,0:T(8,128)(2,1)}, f32[512,128]{1,0:T(8,128)}) custom-call(s32[1,2]{1,0:T(1,128)} %levels.3, f32[512,128]{1,0:T(8,128)} %window_in.1, f32[1024,128]{1,0:T(8,128)} %bitcast.5, bf16[32,3072]{1,0:T(8,128)(2,1)} %w_qkv_in.1), custom_call_target="tpu_custom_call" | custom-call | flops 100000000 | bytes 2000000 | tf_op jit(solution)/shard_map/pack/pallas_call | solution.py:303
  3.0 0.0 copy-start.7
  3.0 0.0 copy-start.1
  3.0 0.0 copy-start.4
  3.0 0.0 copy-start.5
  3.0 11.5 %all-to-all-start = ((bf16[32,64,128]{2,1,0:T(8,128)(2,1)}), bf16[32,64,128]{2,1,0:T(8,128)(2,1)S(1)}, u32[]{:S(2)}, u32[]{:S(2)}) async-start(bf16[32,64,128]{2,1,0:T(8,128)(2,1)} %get-tuple-element.22), calls=%async_computation | async-start | bytes 1048576 | tf_op jit(solution)/shard_map/all_to_all | solution.py:317
  14.6 2.1 %collective-permute-start = (f32[512,128]{1,0:T(8,128)}, f32[512,128]{1,0:T(8,128)S(1)}, u32[]{:S(2)}, u32[]{:S(2)}) collective-permute-start(f32[512,128]{1,0:T(8,128)} %get-tuple-element.23), channel_id=1, source_target_pairs={{16,0},{32,16},{48,32},{64,48},{80,64},{96,80},{112,96},{128,112},... | collective-permute-start | bytes 786440 | tf_op jit(solution)/shard_map/ppermute | solution.py:257
  16.7 10.9 %collective-permute-done.moved = f32[512,128]{1,0:T(8,128)S(1)} collective-permute-done((f32[512,128]{1,0:T(8,128)}, f32[512,128]{1,0:T(8,128)S(1)}, u32[]{:S(2)}, u32[]{:S(2)}) %collective-permute-start) | collective-permute-done | bytes 262176 | tf_op jit(solution)/shard_map/ppermute | solution.py:257
  27.6 0.5 tables.1
  28.2 3.2 %all-to-all-done.received = bf16[32,64,128]{2,1,0:T(8,128)(2,1)S(1)} async-done(((bf16[32,64,128]{2,1,0:T(8,128)(2,1)}), bf16[32,64,128]{2,1,0:T(8,128)(2,1)S(1)}, u32[]{:S(2)}, u32[]{:S(2)}) %all-to-all-start) | async-done | bytes 524320 | tf_op jit(solution)/shard_map/all_to_all | solution.py:317
  31.4 0.4 project.1
  31.8 0.0 copy-start
  31.8 0.0 copy-start.2
  31.8 0.0 copy-start.3
  31.8 15.6 %all_to_all.15.mine = bf16[16,128,128]{2,1,0:T(8,128)(2,1)S(1)} all-to-all(bf16[16,128,128]{2,1,0:T(8,128)(2,1)S(1)} %project.1), channel_id=1, replica_groups={{0,32,1,33,128,160,129,161,256,288,257,289,384,416,385,417},{64,96,65,9..., dimensions={0} | all-to-all | bytes 1048576 | tf_op jit(solution)/shard_map/all_to_all | solution.py:339
  47.4 1.9 %collective-permute-start.1 = (bf16[16,128,128]{2,1,0:T(8,128)(2,1)S(1)}, bf16[16,128,128]{2,1,0:T(8,128)(2,1)S(1)}, u32[]{:S(2)}, u32[]{:S(2)}) collective-permute-start(bf16[16,128,128]{2,1,0:T(8,128)(2,1)S(1)} %all_to_all.15.mine), channel_id=1, source_target_pairs={{0,16},{16,0},{32,48},{48,32},{64,80},{80,64},{96,112},{112,96},{1... | collective-permute-start | bytes 1572872 | tf_op jit(solution)/shard_map/ppermute | solution.py:364
  49.4 0.0 copy-start.8
  49.4 0.0 copy-start.9
  49.4 0.6 copy-done.8
  50.0 0.0 copy-done.9
  50.0 1.6 %before.1 = (bf16[512,256]{1,0:T(8,128)(2,1)S(1)}, f32[512,128]{1,0:T(8,128)S(1)}, f32[512,128]{1,0:T(8,128)S(1)}, bf16[256,128]{1,0:T(8,128)(2,1)S(1)}, f32[3,2...) custom-call(s32[1,2]{1,0:T(1,128)S(1)} %copy-done.8, ...), custom_call_target="tpu_custom_call" | custom-call | flops 400000000 | bytes 4000000 | tf_op jit(solution)/shard_map/before/pallas_call | solution.py:347
  51.6 7.6 %passes.1 = bf16[32,16,128]{2,1,0:T(8,128)(2,1)S(1)} custom-call(bf16[16,128,128]{2,1,0:T(8,128)(2,1)S(1)} %all_to_all.15.mine, bf16[16,128,128]{2,1,0:T(8,128)(2,1)S(1)} %collective-permute-done.1.other, bf16[256,1024]{1,0:T(8,128)(2,1)S(1)} %get-tuple-element.25.embed_in, bf16[512,128]{1,0:T(8,128)(2,1)S(1)} %get-tuple-element.26.residual, ...), custom_call_target="tpu_custom_call" | custom-call | flops 5000000000 | bytes 4000000 | tf_op jit(solution)/shard_map/passes/pallas_call | solution.py:365
  59.2 13.9 %all_to_all.16 = bf16[32,16,128]{2,1,0:T(8,128)(2,1)S(1)} all-to-all(bf16[32,16,128]{2,1,0:T(8,128)(2,1)S(1)} %passes.1), channel_id=1, replica_groups=mesh['frame'=32,'batch'=16] {'frame'}, dimensions={0} | all-to-all | bytes 262144 | tf_op jit(solution)/shard_map/all_to_all | solution.py:377
  73.1 0.7 convert_add_fusion
  (10 shorter events, 0.0 us)
Async XLA Ops:
  0.0 27.6 %copy-start.6 = (bf16[32,256]{1,0:T(8,128)(2,1)S(1)}, bf16[32,256]{1,0:T(8,128)(2,1)}, u32[]{:S(2)}) copy-start(bf16[32,256]{1,0:T(8,128)(2,1)} %constant.4.feats) | copy-start | bytes 49156
  3.0 24.6 %copy-start.7 = (f32[1024]{0:T(1024)S(1)}, f32[1024]{0:T(1024)}, u32[]{:S(2)}) copy-start(f32[1024]{0:T(1024)} %param.19) | copy-start | bytes 12292
  3.0 24.6 %copy-start.1 = (bf16[256,1024]{1,0:T(8,128)(2,1)S(1)}, bf16[256,1024]{1,0:T(8,128)(2,1)}, u32[]{:S(2)}) copy-start(bf16[256,1024]{1,0:T(8,128)(2,1)} %w_level) | copy-start | bytes 1572868
  3.0 24.6 %copy-start.4 = (bf16[128,1024]{1,0:T(8,128)(2,1)S(1)}, bf16[128,1024]{1,0:T(8,128)(2,1)}, u32[]{:S(2)}) copy-start(bf16[128,1024]{1,0:T(8,128)(2,1)} %w_in.1) | copy-start | bytes 786436
  3.0 24.6 %copy-start.5 = (bf16[1024,128]{1,0:T(8,128)(2,1)S(1)}, bf16[1024,128]{1,0:T(8,128)(2,1)}, u32[]{:S(2)}) copy-start(bf16[1024,128]{1,0:T(8,128)(2,1)} %w_res.1) | copy-start | bytes 786436
  3.0 28.3 %all-to-all-start = ((bf16[32,64,128]{2,1,0:T(8,128)(2,1)}), bf16[32,64,128]{2,1,0:T(8,128)(2,1)S(1)}, u32[]{:S(2)}, u32[]{:S(2)}) async-start(bf16[32,64,128]{2,1,0:T(8,128)(2,1)} %get-tuple-element.22), calls=%async_computation | async-start | bytes 1048576 | tf_op jit(solution)/shard_map/all_to_all | solution.py:317
  14.6 13.0 %collective-permute-start = (f32[512,128]{1,0:T(8,128)}, f32[512,128]{1,0:T(8,128)S(1)}, u32[]{:S(2)}, u32[]{:S(2)}) collective-permute-start(f32[512,128]{1,0:T(8,128)} %get-tuple-element.23), channel_id=1, source_target_pairs={{16,0},{32,16},{48,32},{64,48},{80,64},{96,80},{112,96},{128,112},... | collective-permute-start | bytes 786440 | tf_op jit(solution)/shard_map/ppermute | solution.py:257
  31.8 17.6 %copy-start = (f32[512,2,128]{2,1,0:T(2,128)S(1)}, f32[512,2,128]{2,1,0:T(2,128)}, u32[]{:S(2)}) copy-start(f32[512,2,128]{2,1,0:T(2,128)} %param.13) | copy-start | bytes 1572868
  31.8 17.6 %copy-start.2 = (f32[512,128]{1,0:T(8,128)S(1)}, f32[512,128]{1,0:T(8,128)}, u32[]{:S(2)}) copy-start(f32[512,128]{1,0:T(8,128)} %fresh.1) | copy-start | bytes 786436
  31.8 17.6 %copy-start.3 = (bf16[1024,128]{1,0:T(8,128)(2,1)S(1)}, bf16[1024,128]{1,0:T(8,128)(2,1)}, u32[]{:S(2)}) copy-start(bf16[1024,128]{1,0:T(8,128)(2,1)} %w_out_in.1) | copy-start | bytes 786436
  47.4 4.2 %collective-permute-start.1 = (bf16[16,128,128]{2,1,0:T(8,128)(2,1)S(1)}, bf16[16,128,128]{2,1,0:T(8,128)(2,1)S(1)}, u32[]{:S(2)}, u32[]{:S(2)}) collective-permute-start(bf16[16,128,128]{2,1,0:T(8,128)(2,1)S(1)} %all_to_all.15.mine), channel_id=1, source_target_pairs={{0,16},{16,0},{32,48},{48,32},{64,80},{80,64},{96,112},{112,96},{1... | collective-permute-start | bytes 1572872 | tf_op jit(solution)/shard_map/ppermute | solution.py:364
  49.4 0.7 copy-start.8
  49.4 0.7 copy-start.9

commit v3 on v2

--- a/solution.py
+++ b/solution.py
@@ -47,7 +47,7 @@
     return lax.broadcasted_iota(jnp.int32, shape, dim)
 
 
-def pack_kernel(levels, window_in, noise_in, w_qkv_in, out, base_out, window, noise, w_qkv, sems):
+def pack_kernel(levels, window_in, noise_in, w_qkv_in, out, window, noise, w_qkv, sems):
     copies = [
         pltpu.make_async_copy(src, dst, sems.at[k])
         for k, (src, dst) in enumerate(
@@ -92,7 +92,6 @@
     out[:, 32:48, :] = scaled.reshape(FRAMES, POS, C).astype(BF16)
     copies[2].wait()
     base = state + (0.6 * sigma_of(first + 1.0)[:1]) * noise[pl.ds(0, ROWS, stride=2), :]
-    base_out[...] = base
     out[:, 48:64, :] = base.reshape(FRAMES, POS, C).astype(BF16)
 
 
@@ -101,16 +100,30 @@
     return high, (value - high.astype(F32)).astype(BF16)
 
 
-def table_kernel(feats, w_level, w_in, gain, w_res, high, low, embed_in, residual):
+def table_kernel(
+    levels, reach, feats, w_level, w_in, gain, w_res, noise,
+    high, low, embed_in, residual, mask, late,
+):
     emb = dot(feats[...], w_level[...])
     embed_in[0:128, :] = w_in[...]
     embed_in[128:160, :], embed_in[160:192, :] = split(emb)
     embed_in[192:256, :] = jnp.zeros((64, D), BF16)
     scaled = jnp.concatenate([w_in[...].astype(F32), emb], axis=0) * gain[...]
     high[...], low[...] = split(scaled)
-    residual[...] = jnp.zeros((512, C), BF16)
+    residual[...] = jnp.zeros((256, 2 * C), BF16)
     product = dot(high[...], w_res[...]) + dot(low[...], w_res[...])
-    residual[0:160, :], residual[256:416, :] = split(product)
+    residual[0:160, :C], residual[0:160, C:] = split(product)
+    query = iota((SPAN, SPAN), 0)
+    key = iota((SPAN, SPAN), 1)
+    back = jnp.concatenate([jnp.full((GROUP, SPAN), reach[j], jnp.int32) for j in range(FRAMES)], axis=0)
+    allowed = (
+        (query % GROUP == key % GROUP)
+        & (key // GROUP <= query // GROUP)
+        & (key // GROUP >= query // GROUP - back)
+    )
+    mask[...] = jnp.where(allowed, F32(0.0), F32(-1e30))
+    level = jnp.full((8, C), levels[0, 1], jnp.int32).astype(F32)[:1]
+    late[...] = (0.6 * sigma_of(level + 1.0)) * noise[pl.ds(1, ROWS, stride=2), :]
 
 
 def project_kernel(received, high, low, out):
@@ -132,7 +145,8 @@
     hidden = dot(full, embed_in[...])
     scale = lax.rsqrt(jnp.mean(hidden * hidden, axis=-1, keepdims=True) + 1e-06)
     scale = jnp.broadcast_to(scale, (ROWS, C))
-    kept = scale * (dot(full, residual[0:256, :]) + dot(full, residual[256:512, :]))
+    both = dot(full, residual[...])
+    kept = scale * (both[:, :C] + both[:, C:])
     halves = [(full[:, k * C : (k + 1) * C].astype(F32) * scale).astype(BF16) for k in range(2)]
     return jnp.concatenate(halves, axis=1), kept
 
@@ -146,25 +160,10 @@
 
 
 def before_kernel(
-    levels, reach, received, embed_in, residual, fresh, moved, noise, w_out_in,
-    normed, kept, base, hot, scales, mask, entering, w_out, start,
+    received, embed_in, residual, fresh, normed, kept, base, hot, scales, entering
 ):
     place = lax.axis_index("frame")
-    last = jnp.full((8, C), place, jnp.int32)[:1] == FRAMES - 1
-    level = jnp.full((8, C), levels[0, 1], jnp.int32).astype(F32)[:1]
-    late = (0.6 * sigma_of(level + 1.0)) * noise[pl.ds(1, ROWS, stride=2), :]
-    start[...] = jnp.where(last, fresh[...], moved[...]) + late
-    w_out[...] = w_out_in[...]
     entering[...] = fresh[pl.ds(pl.multiple_of(place * POS, POS), POS), :]
-    query = iota((SPAN, SPAN), 0)
-    key = iota((SPAN, SPAN), 1)
-    back = jnp.concatenate([jnp.full((GROUP, SPAN), reach[j], jnp.int32) for j in range(FRAMES)], axis=0)
-    allowed = (
-        (query % GROUP == key % GROUP)
-        & (key // GROUP <= query // GROUP)
-        & (key // GROUP >= query // GROUP - back)
-    )
-    mask[...] = jnp.where(allowed, F32(0.0), F32(-1e30))
     lane = iota((SPAN, HDIM), 1).astype(F32)
     sel_row = iota((HDIM, HDIM), 0)
     hots = []
@@ -186,7 +185,7 @@
 
 
 def passes_kernel(
-    mine, other, embed_in, residual, normed, kept, base, hot, scales, mask, entering, w_out,
+    mine, other, embed_in, residual, mask, w_out, normed, kept, base, hot, scales, entering,
     out, pairs, values, attn,
 ):
     core = lax.axis_index("frame") % 2
@@ -194,11 +193,11 @@
     piece = row // HDIM
     target = row % HDIM // PART * HDIM + (piece + core - 2 * (piece % 2) * core) * PART + row % PART
     pick = (iota((4 * HDIM, 4 * HDIM), 1) == target).astype(F32).astype(BF16)
+    pieces = [[mine[2 * h], other[2 * h], mine[2 * h + 1], other[2 * h + 1]] for h in range(HEADS)]
+    pieces = jnp.concatenate([jnp.concatenate(four, axis=1) for four in pieces], axis=0)
+    in_order = dot(pieces, pick).astype(BF16)
     for h in range(HEADS):
-        pieces = jnp.concatenate(
-            [mine[2 * h], other[2 * h], mine[2 * h + 1], other[2 * h + 1]], axis=1
-        )
-        ordered = dot(pieces, pick).astype(BF16)
+        ordered = in_order[h * C : (h + 1) * C]
         beside = slice(h % 2 * HDIM, (h % 2 + 1) * HDIM)
         pairs[h, 0:128, :] = ordered[:, : 2 * HDIM]
         values[h // 2, 0:128, beside] = ordered[:, 2 * HDIM : 3 * HDIM]
@@ -209,52 +208,62 @@
         values[h // 2, 160:256, beside] = jnp.zeros((96, HDIM), BF16)
     ones = jnp.ones((SPAN, HDIM), BF16)
 
+    def project(normed, h):
+        both = dot(normed, values[h // 2]).astype(BF16) if h % 2 == 0 else None
+        return dot(normed, pairs[h]).astype(BF16), both
+
+    def score(query_key, g):
+        rows = slice(g * SPAN, (g + 1) * SPAN)
+        return mask[...] + lax.dot_general(
+            query_key[rows, :HDIM],
+            query_key[rows, HDIM:],
+            (((1,), (1,)), ((), ())),
+            preferred_element_type=F32,
+        )
+
+    def soften(scores):
+        return jnp.exp2(scores - jnp.max(scores, axis=-1, keepdims=True)).astype(BF16)
+
+    def gather(expo, both, h, g):
+        rows = slice(g * SPAN, (g + 1) * SPAN)
+        value = both[rows, h % 2 * HDIM : (h % 2 + 1) * HDIM]
+        total = dot(expo, jnp.concatenate([value, ones], axis=1))
+        attn[rows, h * HDIM : (h + 1) * HDIM] = (total[:, :HDIM] / total[:, HDIM:]).astype(BF16)
+
     def predict(normed, kept):
-        for h in range(HEADS):
-            query_key = dot(normed, pairs[h]).astype(BF16)
-            if h % 2 == 0:
-                both = dot(normed, values[h // 2]).astype(BF16)
-            for g in range(POS // GROUP):
-                rows = slice(g * SPAN, (g + 1) * SPAN)
-                scores = mask[...] + lax.dot_general(
-                    query_key[rows, :HDIM],
-                    query_key[rows, HDIM:],
-                    (((1,), (1,)), ((), ())),
-                    preferred_element_type=F32,
-                )
-                expo = jnp.exp2(scores - jnp.max(scores, axis=-1, keepdims=True)).astype(BF16)
-                value = both[rows, h % 2 * HDIM : (h % 2 + 1) * HDIM]
-                total = dot(expo, jnp.concatenate([value, ones], axis=1))
-                attn[rows, h * HDIM : (h + 1) * HDIM] = (
-                    total[:, :HDIM] / total[:, HDIM:]
-                ).astype(BF16)
+        steps = range(POS // GROUP)
+        projected, both, scores, expo = {}, {}, {}, {}
+        for now in range(HEADS + 3):
+            if now < HEADS:
+                projected[now], pair = project(normed, now)
+                both[now] = both[now - 1] if pair is None else pair
+            if 0 <= now - 1 < HEADS:
+                scores[now - 1] = [score(projected[now - 1], g) for g in steps]
+            if 0 <= now - 2 < HEADS:
+                expo[now - 2] = [soften(block) for block in scores[now - 2]]
+            if 0 <= now - 3 < HEADS:
+                for g in steps:
+                    gather(expo[now - 3][g], both[now - 3], now - 3, g)
         return kept + dot(attn[...], w_out[...])
 
     def both_groups(block):
         return jnp.concatenate([block] * (POS // GROUP), axis=0)
 
-    def next_slot(block, entering):
+    def next_slot(block):
         parts = []
         for g in range(POS // GROUP):
             parts += [block[g * SPAN + GROUP : (g + 1) * SPAN], entering[g * GROUP : (g + 1) * GROUP]]
         return jnp.concatenate(parts, axis=0)
 
-    moved = both_groups(scales[0]) * predict(normed[...], kept[...])
-    tokens = next_slot(base[...] + moved, entering[...]) * both_groups(scales[2])
-    delta = both_groups(scales[1]) * predict(
+    state = next_slot(base[...] + both_groups(scales[0]) * predict(normed[...], kept[...]))
+    tokens = state * both_groups(scales[2])
+    state += both_groups(scales[1]) * predict(
         *normalised(tokens, both_groups(hot[...]), embed_in, residual)
     )
-    delta += next_slot(moved, jnp.zeros((POS, C), F32))
     parts = [
-        delta[g * SPAN : (g + 1) * SPAN].reshape(FRAMES, 1, GROUP, C) for g in range(POS // GROUP)
+        state[g * SPAN : (g + 1) * SPAN].reshape(FRAMES, 1, GROUP, C) for g in range(POS // GROUP)
     ]
     out[...] = jnp.concatenate(parts, axis=1).reshape(FRAMES, POS, C).astype(BF16)
-
-
-def shifted(block, axis, distance):
-    devices = range(lax.axis_size(axis))
-    route = [(i - distance, i) for i in devices if i - distance in devices]
-    return lax.ppermute(block, axis, route)
 
 
 def struct(shape, dtype):
@@ -300,10 +309,10 @@
 
 def on_device(window, noise, fresh, levels, reach, w_in, w_level, norm_gain, w_qkv, w_out, w_res):
     pairs_of_noise = noise.reshape(2 * ROWS, C)
-    payload, base = call(
+    payload = call(
         pack_kernel,
         "pack",
-        (struct((FRAMES, 64, C), BF16), struct((ROWS, C), F32)),
+        struct((FRAMES, 64, C), BF16),
         [SMEM] + [HBM] * 3,
         (10**8, 2 * 10**6),
         [
@@ -315,20 +324,23 @@
         None,
     )(levels, window, pairs_of_noise, w_qkv)
     received = lax.all_to_all(payload, "frame", split_axis=0, concat_axis=0, tiled=True)
-    moved = shifted(base, "frame", -1)
-    moved, w_level = lax.optimization_barrier((moved, w_level))
-    high, low, embed_in, residual = call(
+    high, low, embed_in, residual, mask, late = call(
         table_kernel,
         "tables",
         (
             struct((160, D), BF16),
             struct((160, D), BF16),
             struct((256, D), BF16),
-            struct((512, C), BF16),
+            struct((256, 2 * C), BF16),
+            struct((SPAN, SPAN), F32),
+            struct((ROWS, C), F32),
         ),
-        [VMEM] * 5,
+        [SMEM, SMEM] + [VMEM] * 6,
         (10**8, 3 * 10**6),
-    )(feats_table(), w_level, w_in, norm_gain.reshape(1, D), w_res)
+    )(
+        levels, reach, feats_table(), w_level, w_in, norm_gain.reshape(1, D), w_res,
+        pairs_of_noise,
+    )
     packed = call(
         project_kernel,
         "project",
@@ -344,7 +356,7 @@
         tiled=True,
         axis_index_groups=spread_groups(lax.axis_size("batch")),
     )
-    *prepared, start = call(
+    prepared = call(
         before_kernel,
         "before",
         (
@@ -353,16 +365,13 @@
             struct((ROWS, C), F32),
             struct((SPAN, C), BF16),
             struct((3, SPAN, C), F32),
-            struct((SPAN, SPAN), F32),
             struct((POS, C), F32),
-            struct((D, C), BF16),
-            struct((ROWS, C), F32),
         ),
-        [SMEM, SMEM] + [VMEM] * 7,
+        [VMEM] * 4,
         (4 * 10**8, 4 * 10**6),
-    )(levels, reach, received, embed_in, residual, fresh, moved, pairs_of_noise, w_out)
+    )(received, embed_in, residual, fresh)
     other = lax.ppermute(mine, "frame", [(i, i ^ 1) for i in range(FRAMES)])
-    delta = call(
+    state = call(
         passes_kernel,
         "passes",
         struct((FRAMES, POS, C), BF16),
@@ -373,9 +382,9 @@
             pltpu.VMEM((HEADS // 2, 256, 2 * HDIM), BF16),
             pltpu.VMEM((ROWS, HEADS * HDIM), BF16),
         ],
-    )(mine, other, embed_in, residual, *prepared)
-    back = lax.all_to_all(delta, "frame", split_axis=0, concat_axis=0, tiled=True)
-    return start + back.reshape(ROWS, C).astype(F32)
+    )(mine, other, embed_in, residual, mask, w_out, *prepared)
+    back = lax.all_to_all(state, "frame", split_axis=0, concat_axis=0, tiled=True)
+    return late + back.reshape(ROWS, C).astype(F32)
 
 
 def solution(mesh):

time: 74.2 us -> 69 us (0.930)
  blocking collectives: 29.5 us -> 26 us
  Pallas kernels: 13 us -> 11 us
  starting transfers between devices: 15.6 us -> 14.4 us
  waiting for transfers between devices: 14.1 us -> 14.9 us
  local copies, waits for them, and re-layouts: 0.68 us -> 1.44 us
    all_to_all x1, waiting for transfers between devices: 3.21 us -> 14.2 us  [on_device(): lax.all_to_all(payload, 'frame', split_axis=0, concat_axis=0, tiled=True)]
    ppermute x1 -> x0, waiting for transfers between devices: 10.9 us -> none  [shifted(): return lax.ppermute(block, axis, route)]
    all_to_all x1, blocking collectives: 15.6 us -> 13.4 us  [on_device(): lax.all_to_all(packed, ('frame', 'batch'), split_axis=0, concat_axis=0, t...]
    ppermute x1 -> x0, starting transfers between devices: 2.14 us -> none  [shifted(): return lax.ppermute(block, axis, route)]
    pallas_call x1, Pallas kernels: 7.56 us -> 5.79 us  [on_device(): call(passes_kernel, 'passes', struct((FRAMES, POS, C), BF16), [VMEM] * 12...]
    all_to_all x1, blocking collectives: 13.9 us -> 12.6 us  [on_device(): lax.all_to_all(state, 'frame', split_axis=0, concat_axis=0, tiled=True)]
    ppermute x1, starting transfers between devices: 1.91 us -> 2.86 us  [on_device(): other = lax.ppermute(mine, 'frame', [(i, i ^ 1) for i in range(FRAMES)])]
    pallas_call x1, Pallas kernels: 1.57 us -> 0.79 us  [on_device(): call(before_kernel, 'before', (struct((ROWS, 2 * C), BF16), struct((ROWS,...]
  transfers between devices with their start and end apart: 3 -> 2, of which waited for: 2 -> 2; matrix products, arithmetic and copies ran while one was open for 0% -> 0% of each run, Pallas kernels for 3% -> 3%
where the time goes in v3:
time: 69 us; the launch traced here: 68.7 us
  blocking collectives  26 us (38%)
  waiting for transfers between devices  14.9 us (22%)
  starting transfers between devices  14.4 us (21%)
  Pallas kernels  11 us (16%)
  local copies, waits for them, and re-layouts  1.44 us (2%)
  other arithmetic  0.73 us (1%)
    all_to_all x1, waiting for transfers between devices, on_device(): lax.all_to_all(payload, 'frame', split_axis=0, concat_axis=0, tiled=True)  14.2 us
    all_to_all x1, blocking collectives, on_device(): lax.all_to_all(packed, ('frame', 'batch'), split_axis=0, concat_axis=0, t...  13.4 us
    all_to_all x1, blocking collectives, on_device(): lax.all_to_all(state, 'frame', split_axis=0, concat_axis=0, tiled=True)  12.6 us
    all_to_all x1, starting transfers between devices, on_device(): lax.all_to_all(payload, 'frame', split_axis=0, concat_axis=0, tiled=True)  11.5 us
    pallas_call x1, Pallas kernels, on_device(): call(passes_kernel, 'passes', struct((FRAMES, POS, C), BF16), [VMEM] * 12...  5.79 us
    pallas_call x1, Pallas kernels, on_device(): call(pack_kernel, 'pack', struct((FRAMES, 64, C), BF16), [SMEM] + [HBM] *...  2.88 us
    ppermute x1, starting transfers between devices, on_device(): other = lax.ppermute(mine, 'frame', [(i, i ^ 1) for i in range(FRAMES)])  2.86 us
    unnamed x24, local copies, waits for them, and re-layouts  1.44 us
  transfers between devices with their start and end apart: 2, of which 2 were waited for; matrix products, arithmetic and copies ran while one was open for 0% of the time, Pallas kernels for 3%

profile of v3, /device:TPU:1, one launch (start us, length us, event | category | flops | bytes accessed | tf_op | source)
XLA Modules:
  0.0 68.7 jit_solution(7091934818332407487)
XLA Ops:
  0.0 2.9 %pack.1 = bf16[32,64,128]{2,1,0:T(8,128)(2,1)} custom-call(s32[1,2]{1,0:T(1,128)} %levels.3, f32[512,128]{1,0:T(8,128)} %window_in.1, f32[1024,128]{1,0:T(8,128)} %bitcast.5, bf16[32,3072]{1,0:T(8,128)(2,1)} %w_qkv_in.1), custom_call_target="tpu_custom_call" | custom-call | flops 100000000 | bytes 2000000 | tf_op jit(solution)/shard_map/pack/pallas_call | solution.py:312
  2.9 0.0 copy-start
  2.9 0.0 copy-start.1
  2.9 11.5 %all-to-all-start = ((bf16[32,64,128]{2,1,0:T(8,128)(2,1)}), bf16[32,64,128]{2,1,0:T(8,128)(2,1)S(1)}, u32[]{:S(2)}, u32[]{:S(2)}) async-start(bf16[32,64,128]{2,1,0:T(8,128)(2,1)} %pack.1), calls=%async_computation | async-start | bytes 1048576 | tf_op jit(solution)/shard_map/all_to_all | solution.py:326
  14.5 0.0 copy-start.6
  14.5 0.0 copy-start.7
  14.5 0.0 copy-done.2
  14.5 0.0 copy-done.3
  14.5 0.0 copy-done.4
  14.6 0.6 copy-done.6
  15.1 0.0 copy-done.7
  15.1 1.1 %tables.1 = (bf16[160,1024]{1,0:T(8,128)(2,1)S(1)}, bf16[160,1024]{1,0:T(8,128)(2,1)S(1)}, bf16[256,1024]{1,0:T(8,128)(2,1)S(1)}, bf16[256,256]{1,0:T(8,128)(2,1...) custom-call(s32[1,2]{1,0:T(1,128)S(1)} %copy-done.6, s32[32]{0:T(128)S(1)} %copy-done.7, ...), custom_call_target="tpu_custom_call" | custom-call | flops 100000000 | bytes 3000000 | tf_op jit(solution)/shard_map/tables/pallas_call | solution.py:327
  16.3 0.8 %copy-done.8 = bf16[256,1024]{1,0:T(8,128)(2,1)} copy-done((bf16[256,1024]{1,0:T(8,128)(2,1)}, bf16[256,1024]{1,0:T(8,128)(2,1)S(1)}, u32[]{:S(2)}) %copy-start.8) | copy-done | bytes 524312
  17.1 14.2 %all-to-all-done.received = bf16[32,64,128]{2,1,0:T(8,128)(2,1)S(1)} async-done(((bf16[32,64,128]{2,1,0:T(8,128)(2,1)}), bf16[32,64,128]{2,1,0:T(8,128)(2,1)S(1)}, u32[]{:S(2)}, u32[]{:S(2)}) %all-to-all-start) | async-done | bytes 524320 | tf_op jit(solution)/shard_map/all_to_all | solution.py:326
  31.3 0.4 project.1
  31.7 0.0 copy-start.10
  31.7 13.4 %all_to_all.15.mine = bf16[16,128,128]{2,1,0:T(8,128)(2,1)S(1)} all-to-all(bf16[16,128,128]{2,1,0:T(8,128)(2,1)S(1)} %project.1), channel_id=1, replica_groups={{0,32,1,33,128,160,129,161,256,288,257,289,384,416,385,417},{64,96,65,9..., dimensions={0} | all-to-all | bytes 1048576 | tf_op jit(solution)/shard_map/all_to_all | solution.py:351
  45.2 2.9 %collective-permute-start = (bf16[16,128,128]{2,1,0:T(8,128)(2,1)S(1)}, bf16[16,128,128]{2,1,0:T(8,128)(2,1)S(1)}, u32[]{:S(2)}, u32[]{:S(2)}) collective-permute-start(bf16[16,128,128]{2,1,0:T(8,128)(2,1)S(1)} %all_to_all.15.mine), channel_id=1, source_target_pairs={{0,16},{16,0},{32,48},{48,32},{64,80},{80,64},{96,112},{112,96},{1... | collective-permute-start | bytes 1572872 | tf_op jit(solution)/shard_map/ppermute | solution.py:373
  48.0 0.0 copy-start.11
  48.0 0.8 %before.1 = (bf16[512,256]{1,0:T(8,128)(2,1)S(1)}, f32[512,128]{1,0:T(8,128)S(1)}, f32[512,128]{1,0:T(8,128)S(1)}, bf16[256,128]{1,0:T(8,128)(2,1)S(1)}, f32[3,2...) custom-call(bf16[32,64,128]{2,1,0:T(8,128)(2,1)S(1)} %all-to-all-done.received, bf16[256,1024]{1,0:T(8,128)(2,1)S(1)} %copy-done.9, ...), custom_call_target="tpu_custom_call" | custom-call | flops 400000000 | bytes 4000000 | tf_op jit(solution)/shard_map/before/pallas_call | solution.py:359
  48.8 0.7 collective-permute-done.other
  49.5 5.8 %passes.1 = bf16[32,16,128]{2,1,0:T(8,128)(2,1)S(1)} custom-call(bf16[16,128,128]{2,1,0:T(8,128)(2,1)S(1)} %all_to_all.15.mine, bf16[16,128,128]{2,1,0:T(8,128)(2,1)S(1)} %collective-permute-done.other, bf16[256,1024]{1,0:T(8,128)(2,1)S(1)} %copy-done.9, bf16[256,256]{1,0:T(8,128)(2,1)S(1)} %get-tuple-element.21.residual, ...), custom_call_target="tpu_custom_call" | custom-call | flops 5000000000 | bytes 4000000 | tf_op jit(solution)/shard_map/passes/pallas_call | solution.py:374
  55.3 12.6 %all_to_all.16 = bf16[32,16,128]{2,1,0:T(8,128)(2,1)S(1)} all-to-all(bf16[32,16,128]{2,1,0:T(8,128)(2,1)S(1)} %passes.1), channel_id=1, replica_groups=mesh['frame'=32,'batch'=16] {'frame'}, dimensions={0} | all-to-all | bytes 262144 | tf_op jit(solution)/shard_map/all_to_all | solution.py:386
  67.9 0.7 %convert_add_fusion = f32[512,128]{1,0:T(8,128)} fusion(f32[512,128]{1,0:T(8,128)S(1)} %get-tuple-element.17, bf16[32,16,128]{2,1,0:T(8,128)(2,1)S(1)} %all_to_all.16), kind=kLoop, calls=%fused_computation | loop fusion | flops 131072 | bytes 655360 | tf_op jit(solution)/shard_map/add | solution.py:387
  (12 shorter events, 0.0 us)
Async XLA Ops:
  0.0 14.5 %copy-start.2 = (bf16[128,1024]{1,0:T(8,128)(2,1)S(1)}, bf16[128,1024]{1,0:T(8,128)(2,1)}, u32[]{:S(2)}) copy-start(bf16[128,1024]{1,0:T(8,128)(2,1)} %w_in.1) | copy-start | bytes 786436
  0.0 14.5 %copy-start.3 = (bf16[1024,128]{1,0:T(8,128)(2,1)S(1)}, bf16[1024,128]{1,0:T(8,128)(2,1)}, u32[]{:S(2)}) copy-start(bf16[1024,128]{1,0:T(8,128)(2,1)} %w_res.1) | copy-start | bytes 786436
  0.0 14.5 %copy-start.4 = (bf16[32,256]{1,0:T(8,128)(2,1)S(1)}, bf16[32,256]{1,0:T(8,128)(2,1)}, u32[]{:S(2)}) copy-start(bf16[32,256]{1,0:T(8,128)(2,1)} %constant.4.feats) | copy-start | bytes 49156
  0.0 14.5 %copy-start.5 = (f32[1024]{0:T(1024)S(1)}, f32[1024]{0:T(1024)}, u32[]{:S(2)}) copy-start(f32[1024]{0:T(1024)} %param.19) | copy-start | bytes 12292
  2.9 11.6 %copy-start = (f32[512,2,128]{2,1,0:T(2,128)S(1)}, f32[512,2,128]{2,1,0:T(2,128)}, u32[]{:S(2)}) copy-start(f32[512,2,128]{2,1,0:T(2,128)} %param.13) | copy-start | bytes 1572868
  2.9 11.6 %copy-start.1 = (bf16[256,1024]{1,0:T(8,128)(2,1)S(1)}, bf16[256,1024]{1,0:T(8,128)(2,1)}, u32[]{:S(2)}) copy-start(bf16[256,1024]{1,0:T(8,128)(2,1)} %w_level.1) | copy-start | bytes 1572868
  2.9 28.3 %all-to-all-start = ((bf16[32,64,128]{2,1,0:T(8,128)(2,1)}), bf16[32,64,128]{2,1,0:T(8,128)(2,1)S(1)}, u32[]{:S(2)}, u32[]{:S(2)}) async-start(bf16[32,64,128]{2,1,0:T(8,128)(2,1)} %pack.1), calls=%async_computation | async-start | bytes 1048576 | tf_op jit(solution)/shard_map/all_to_all | solution.py:326
  14.5 0.7 copy-start.6
  14.5 0.7 copy-start.7
  16.3 0.8 %copy-start.8 = (bf16[256,1024]{1,0:T(8,128)(2,1)}, bf16[256,1024]{1,0:T(8,128)(2,1)S(1)}, u32[]{:S(2)}) copy-start(bf16[256,1024]{1,0:T(8,128)(2,1)S(1)} %get-tuple-element.20.embed_in) | copy-start | bytes 1572868
  31.7 16.3 %copy-start.9 = (bf16[256,1024]{1,0:T(8,128)(2,1)S(1)}, bf16[256,1024]{1,0:T(8,128)(2,1)}, u32[]{:S(2)}) copy-start(bf16[256,1024]{1,0:T(8,128)(2,1)} %copy-done.8) | copy-start | bytes 1572868
  31.7 16.3 %copy-start.10 = (f32[512,128]{1,0:T(8,128)S(1)}, f32[512,128]{1,0:T(8,128)}, u32[]{:S(2)}) copy-start(f32[512,128]{1,0:T(8,128)} %fresh.1) | copy-start | bytes 786436
  45.2 4.4 %collective-permute-start = (bf16[16,128,128]{2,1,0:T(8,128)(2,1)S(1)}, bf16[16,128,128]{2,1,0:T(8,128)(2,1)S(1)}, u32[]{:S(2)}, u32[]{:S(2)}) collective-permute-start(bf16[16,128,128]{2,1,0:T(8,128)(2,1)S(1)} %all_to_all.15.mine), channel_id=1, source_target_pairs={{0,16},{16,0},{32,48},{48,32},{64,80},{80,64},{96,112},{112,96},{1... | collective-permute-start | bytes 1572872 | tf_op jit(solution)/shard_map/ppermute | solution.py:373
  48.0 1.5 %copy-start.11 = (bf16[1024,128]{1,0:T(8,128)(2,1)S(1)}, bf16[1024,128]{1,0:T(8,128)(2,1)}, u32[]{:S(2)}) copy-start(bf16[1024,128]{1,0:T(8,128)(2,1)} %w_out.1) | copy-start | bytes 786436

commit v4 on v3

--- a/solution.py
+++ b/solution.py
@@ -9,6 +9,7 @@
 from jax.sharding import PartitionSpec as P
 
 HEADS = 8
+HALF = HEADS // 2
 HDIM = 128
 C = 128
 D = 1024
@@ -58,34 +59,30 @@
         copy.start()
     first = jnp.full((8, C), levels[0, 0], jnp.int32).astype(F32)
     second = jnp.full((8, C), levels[0, 1], jnp.int32).astype(F32)
+    odd = lax.axis_index("batch") % 2
     row = iota((3 * HDIM, 1), 0)
-    target = (row % HDIM) // PART * HDIM + row // HDIM * PART + row % PART
-    pick = (iota((3 * HDIM, 4 * HDIM), 1) == target).astype(F32).astype(BF16)
+    target = (row % HDIM // PART - 2 * odd) * HDIM + row // HDIM * PART + row % PART
+    pick = (iota((3 * HDIM, 2 * HDIM), 1) == target).astype(F32).astype(BF16)
     lane = iota((PART, HDIM), 1)
     sigma = sigma_of(first)[:1]
-    odd = lax.axis_index("batch") % 2
     copies[0].wait()
     stacked = jnp.concatenate(
         [
             jnp.concatenate(
-                [
-                    w_qkv[:, pl.ds(pl.multiple_of((s * HEADS + 2 * x + odd) * HDIM, HDIM), HDIM)]
-                    for s in range(3)
-                ],
-                axis=1,
+                [w_qkv[:, s * D + h * HDIM : s * D + (h + 1) * HDIM] for s in range(3)], axis=1
             )
-            for x in range(4)
+            for h in range(HEADS)
         ],
         axis=0,
     )
     pieces = dot(stacked, pick)
-    for x in range(4):
-        for i in range(4):
-            piece = pieces[x * PART : (x + 1) * PART, i * HDIM : (i + 1) * HDIM]
+    for h in range(HEADS):
+        for i in range(2):
+            piece = pieces[h * PART : (h + 1) * PART, i * HDIM : (i + 1) * HDIM]
             piece = jnp.where(lane == 96, first[:1], jnp.where(lane == 97, second[:1], piece))
             piece = piece.astype(BF16)
-            out[x * 8 + i, 0:32, :] = piece
-            out[x * 8 + i + 4, 0:32, :] = piece
+            for z in (i, i + 2):
+                out[h // 2 * 8 + z * 2 + h % 2, 0:32, :] = piece
     copies[1].wait()
     state = window[...]
     scaled = state / jnp.sqrt(1.0 + sigma * sigma)
@@ -159,8 +156,70 @@
     )
 
 
+def sort_columns(held, pairs, values):
+    row = iota((4 * HDIM, 1), 0)
+    target = row % HDIM // PART * HDIM + row // HDIM * PART + row % PART
+    pick = (iota((4 * HDIM, 4 * HDIM), 1) == target).astype(F32).astype(BF16)
+    pieces = [jnp.concatenate([held[4 * k + i] for i in range(4)], axis=1) for k in range(HALF)]
+    in_order = dot(jnp.concatenate(pieces, axis=0), pick).astype(BF16)
+    for k in range(HALF):
+        ordered = in_order[k * C : (k + 1) * C]
+        beside = slice(k % 2 * HDIM, (k % 2 + 1) * HDIM)
+        pairs[k, 0:128, :] = ordered[:, : 2 * HDIM]
+        values[k // 2, 0:128, beside] = ordered[:, 2 * HDIM : 3 * HDIM]
+        pairs[k, 128:160, :HDIM] = ordered[0:32, 3 * HDIM :]
+        pairs[k, 128:160, HDIM:] = ordered[32:64, 3 * HDIM :]
+        values[k // 2, 128:160, beside] = ordered[64:96, 3 * HDIM :]
+        pairs[k, 160:256, :] = jnp.zeros((96, 2 * HDIM), BF16)
+        values[k // 2, 160:256, beside] = jnp.zeros((96, HDIM), BF16)
+
+
+def project(normed, weights):
+    return dot(normed, weights).astype(BF16)
+
+
+def projected_before(normed, rows):
+    return rows
+
+
+def attend(normed, heads, mask, attn):
+    ones = jnp.ones((SPAN, HDIM), BF16)
+    groups = [slice(g * SPAN, (g + 1) * SPAN) for g in range(POS // GROUP)]
+    projected, both, scores, expo = {}, {}, {}, {}
+    for now in range(len(heads) + 3):
+        if now < len(heads):
+            pairs, values, k, projects = heads[now]
+            both[now] = both[now - 1] if k % 2 else projects(normed, values[k // 2])
+            projected[now] = projects(normed, pairs[k])
+        if 0 <= now - 1 < len(heads):
+            scores[now - 1] = [
+                mask[...]
+                + lax.dot_general(
+                    projected[now - 1][rows, :HDIM],
+                    projected[now - 1][rows, HDIM:],
+                    (((1,), (1,)), ((), ())),
+                    preferred_element_type=F32,
+                )
+                for rows in groups
+            ]
+        if 0 <= now - 2 < len(heads):
+            expo[now - 2] = [
+                jnp.exp2(block - jnp.max(block, axis=-1, keepdims=True)).astype(BF16)
+                for block in scores[now - 2]
+            ]
+        if 0 <= now - 3 < len(heads):
+            h = now - 3
+            for rows, weights in zip(groups, expo[h]):
+                value = both[h][rows, h % 2 * HDIM : (h % 2 + 1) * HDIM]
+                total = dot(weights, jnp.concatenate([value, ones], axis=1))
+                attn[rows, h * HDIM : (h + 1) * HDIM] = (
+                    total[:, :HDIM] / total[:, HDIM:]
+                ).astype(BF16)
+
+
 def before_kernel(
-    received, embed_in, residual, fresh, normed, kept, base, hot, scales, entering
+    received, mine, embed_in, residual, w_out, fresh,
+    normed, kept, base, hot, scales, entering, pairs, values, first_pairs, first_values, w_sorted,
 ):
     place = lax.axis_index("frame")
     entering[...] = fresh[pl.ds(pl.multiple_of(place * POS, POS), POS), :]
@@ -179,72 +238,31 @@
     hot[...] = hots[1]
     tokens = groups_of(received[:, 32:48, :])
     base[...] = groups_of(received[:, 48:64, :])
-    normed[...], kept[...] = normalised(
+    unit, kept[...] = normalised(
         tokens, jnp.concatenate([hots[0], hots[0]], axis=0), embed_in, residual
     )
+    normed[...] = unit
+    for k in range(HEADS):
+        head = 2 * (k % HALF) + (place + k // HALF) % 2
+        rows = pl.ds(pl.multiple_of(head * HDIM, HDIM), HDIM)
+        w_sorted[k * HDIM : (k + 1) * HDIM, :] = w_out[rows, :]
+    sort_columns(mine, pairs, values)
+    for k in range(HALF):
+        first_pairs[k] = project(unit, pairs[k])
+    for k in range(HALF // 2):
+        first_values[k] = project(unit, values[k])
 
 
 def passes_kernel(
-    mine, other, embed_in, residual, mask, w_out, normed, kept, base, hot, scales, entering,
+    other, embed_in, residual, mask,
+    normed, kept, base, hot, scales, entering, own_pairs, own_values,
+    first_pairs, first_values, w_sorted,
     out, pairs, values, attn,
 ):
-    core = lax.axis_index("frame") % 2
-    row = iota((4 * HDIM, 1), 0)
-    piece = row // HDIM
-    target = row % HDIM // PART * HDIM + (piece + core - 2 * (piece % 2) * core) * PART + row % PART
-    pick = (iota((4 * HDIM, 4 * HDIM), 1) == target).astype(F32).astype(BF16)
-    pieces = [[mine[2 * h], other[2 * h], mine[2 * h + 1], other[2 * h + 1]] for h in range(HEADS)]
-    pieces = jnp.concatenate([jnp.concatenate(four, axis=1) for four in pieces], axis=0)
-    in_order = dot(pieces, pick).astype(BF16)
-    for h in range(HEADS):
-        ordered = in_order[h * C : (h + 1) * C]
-        beside = slice(h % 2 * HDIM, (h % 2 + 1) * HDIM)
-        pairs[h, 0:128, :] = ordered[:, : 2 * HDIM]
-        values[h // 2, 0:128, beside] = ordered[:, 2 * HDIM : 3 * HDIM]
-        pairs[h, 128:160, :HDIM] = ordered[0:32, 3 * HDIM :]
-        pairs[h, 128:160, HDIM:] = ordered[32:64, 3 * HDIM :]
-        values[h // 2, 128:160, beside] = ordered[64:96, 3 * HDIM :]
-        pairs[h, 160:256, :] = jnp.zeros((96, 2 * HDIM), BF16)
-        values[h // 2, 160:256, beside] = jnp.zeros((96, HDIM), BF16)
-    ones = jnp.ones((SPAN, HDIM), BF16)
-
-    def project(normed, h):
-        both = dot(normed, values[h // 2]).astype(BF16) if h % 2 == 0 else None
-        return dot(normed, pairs[h]).astype(BF16), both
-
-    def score(query_key, g):
-        rows = slice(g * SPAN, (g + 1) * SPAN)
-        return mask[...] + lax.dot_general(
-            query_key[rows, :HDIM],
-            query_key[rows, HDIM:],
-            (((1,), (1,)), ((), ())),
-            preferred_element_type=F32,
-        )
-
-    def soften(scores):
-        return jnp.exp2(scores - jnp.max(scores, axis=-1, keepdims=True)).astype(BF16)
-
-    def gather(expo, both, h, g):
-        rows = slice(g * SPAN, (g + 1) * SPAN)
-        value = both[rows, h % 2 * HDIM : (h % 2 + 1) * HDIM]
-        total = dot(expo, jnp.concatenate([value, ones], axis=1))
-        attn[rows, h * HDIM : (h + 1) * HDIM] = (total[:, :HDIM] / total[:, HDIM:]).astype(BF16)
-
-    def predict(normed, kept):
-        steps = range(POS // GROUP)
-        projected, both, scores, expo = {}, {}, {}, {}
-        for now in range(HEADS + 3):
-            if now < HEADS:
-                projected[now], pair = project(normed, now)
-                both[now] = both[now - 1] if pair is None else pair
-            if 0 <= now - 1 < HEADS:
-                scores[now - 1] = [score(projected[now - 1], g) for g in steps]
-            if 0 <= now - 2 < HEADS:
-                expo[now - 2] = [soften(block) for block in scores[now - 2]]
-            if 0 <= now - 3 < HEADS:
-                for g in steps:
-                    gather(expo[now - 3][g], both[now - 3], now - 3, g)
-        return kept + dot(attn[...], w_out[...])
+    sort_columns(other, pairs, values)
+    first = [(first_pairs, first_values, k, projected_before) for k in range(HALF)]
+    own = [(own_pairs, own_values, k, project) for k in range(HALF)]
+    others = [(pairs, values, k, project) for k in range(HALF)]
 
     def both_groups(block):
         return jnp.concatenate([block] * (POS // GROUP), axis=0)
@@ -255,11 +273,15 @@
             parts += [block[g * SPAN + GROUP : (g + 1) * SPAN], entering[g * GROUP : (g + 1) * GROUP]]
         return jnp.concatenate(parts, axis=0)
 
-    state = next_slot(base[...] + both_groups(scales[0]) * predict(normed[...], kept[...]))
+    attend(normed[...], first + others, mask, attn)
+    groups = [slice(g * SPAN, (g + 1) * SPAN) for g in range(POS // GROUP)]
+    preds = [kept[rows, :] + dot(attn[rows, :], w_sorted[...]) for rows in groups]
+    pred = jnp.concatenate(preds, axis=0)
+    state = next_slot(base[...] + both_groups(scales[0]) * pred)
     tokens = state * both_groups(scales[2])
-    state += both_groups(scales[1]) * predict(
-        *normalised(tokens, both_groups(hot[...]), embed_in, residual)
-    )
+    unit, pred = normalised(tokens, both_groups(hot[...]), embed_in, residual)
+    attend(unit, own + others, mask, attn)
+    state += both_groups(scales[1]) * (pred + dot(attn[...], w_sorted[...]))
     parts = [
         state[g * SPAN : (g + 1) * SPAN].reshape(FRAMES, 1, GROUP, C) for g in range(POS // GROUP)
     ]
@@ -366,23 +388,28 @@
             struct((SPAN, C), BF16),
             struct((3, SPAN, C), F32),
             struct((POS, C), F32),
+            struct((HALF, 256, 2 * HDIM), BF16),
+            struct((HALF // 2, 256, 2 * HDIM), BF16),
+            struct((HALF, ROWS, 2 * HDIM), BF16),
+            struct((HALF // 2, ROWS, 2 * HDIM), BF16),
+            struct((D, C), BF16),
         ),
-        [VMEM] * 4,
-        (4 * 10**8, 4 * 10**6),
-    )(received, embed_in, residual, fresh)
+        [VMEM] * 6,
+        (10**9, 6 * 10**6),
+    )(received, mine, embed_in, residual, w_out, fresh)
     other = lax.ppermute(mine, "frame", [(i, i ^ 1) for i in range(FRAMES)])
     state = call(
         passes_kernel,
         "passes",
         struct((FRAMES, POS, C), BF16),
-        [VMEM] * 12,
+        [VMEM] * 15,
         (5 * 10**9, 4 * 10**6),
         [
-            pltpu.VMEM((HEADS, 256, 2 * HDIM), BF16),
-            pltpu.VMEM((HEADS // 2, 256, 2 * HDIM), BF16),
+            pltpu.VMEM((HALF, 256, 2 * HDIM), BF16),
+            pltpu.VMEM((HALF // 2, 256, 2 * HDIM), BF16),
             pltpu.VMEM((ROWS, HEADS * HDIM), BF16),
         ],
-    )(mine, other, embed_in, residual, mask, w_out, *prepared)
+    )(other, embed_in, residual, mask, *prepared)
     back = lax.all_to_all(state, "frame", split_axis=0, concat_axis=0, tiled=True)
     return late + back.reshape(ROWS, C).astype(F32)
 

time: 69 us -> 68.4 us (level)
  waiting for transfers between devices: 14.9 us -> 14.2 us
    pallas_call x1, Pallas kernels: 0.79 us -> 1.52 us  [on_device(): call(before_kernel, 'before', (struct((ROWS, 2 * C), BF16), struct((ROWS,...]
  transfers between devices with their start and end apart: 2 -> 2, of which waited for: 2 -> 1; matrix products, arithmetic and copies ran while one was open for 0% -> 0% of each run, Pallas kernels for 3% -> 4%
where the time goes in v4:
time: 68.4 us; the launch traced here: 68 us
  blocking collectives  26 us (38%)
  starting transfers between devices  14.4 us (21%)
  waiting for transfers between devices  14.2 us (21%)
  Pallas kernels  11.1 us (16%)
  local copies, waits for them, and re-layouts  1.44 us (2%)
  other arithmetic  0.73 us (1%)
    all_to_all x1, waiting for transfers between devices, on_device(): lax.all_to_all(payload, 'frame', split_axis=0, concat_axis=0, tiled=True)  14.2 us
    all_to_all x1, blocking collectives, on_device(): lax.all_to_all(packed, ('frame', 'batch'), split_axis=0, concat_axis=0, t...  13.4 us
    all_to_all x1, blocking collectives, on_device(): lax.all_to_all(state, 'frame', split_axis=0, concat_axis=0, tiled=True)  12.6 us
    all_to_all x1, starting transfers between devices, on_device(): lax.all_to_all(payload, 'frame', split_axis=0, concat_axis=0, tiled=True)  11.5 us
    pallas_call x1, Pallas kernels, on_device(): call(passes_kernel, 'passes', struct((FRAMES, POS, C), BF16), [VMEM] * 15...  5.12 us
    pallas_call x1, Pallas kernels, on_device(): call(pack_kernel, 'pack', struct((FRAMES, 64, C), BF16), [SMEM] + [HBM] *...  2.88 us
    ppermute x1, starting transfers between devices, on_device(): other = lax.ppermute(mine, 'frame', [(i, i ^ 1) for i in range(FRAMES)])  2.86 us
    pallas_call x1, Pallas kernels, on_device(): call(before_kernel, 'before', (struct((ROWS, 2 * C), BF16), struct((ROWS,...  1.52 us
  transfers between devices with their start and end apart: 2, of which 1 were waited for; matrix products, arithmetic and copies ran while one was open for 0% of the time, Pallas kernels for 4%

profile of v4, /device:TPU:1, one launch (start us, length us, event | category | flops | bytes accessed | tf_op | source)
XLA Modules:
  0.0 68.0 jit_solution(10663076304934293400)
XLA Ops:
  0.0 2.9 %pack.1 = bf16[32,64,128]{2,1,0:T(8,128)(2,1)} custom-call(s32[1,2]{1,0:T(1,128)} %levels.3, f32[512,128]{1,0:T(8,128)} %window_in.1, f32[1024,128]{1,0:T(8,128)} %bitcast.5, bf16[32,3072]{1,0:T(8,128)(2,1)} %w_qkv_in.1), custom_call_target="tpu_custom_call" | custom-call | flops 100000000 | bytes 2000000 | tf_op jit(solution)/shard_map/pack/pallas_call | solution.py:334
  2.9 0.0 copy-start
  2.9 0.0 copy-start.1
  2.9 11.5 %all-to-all-start = ((bf16[32,64,128]{2,1,0:T(8,128)(2,1)}), bf16[32,64,128]{2,1,0:T(8,128)(2,1)S(1)}, u32[]{:S(2)}, u32[]{:S(2)}) async-start(bf16[32,64,128]{2,1,0:T(8,128)(2,1)} %pack.1), calls=%async_computation | async-start | bytes 1048576 | tf_op jit(solution)/shard_map/all_to_all | solution.py:348
  14.5 0.0 copy-start.6
  14.5 0.0 copy-start.7
  14.5 0.0 copy-done.2
  14.5 0.0 copy-done.3
  14.5 0.0 copy-done.4
  14.6 0.6 copy-done.6
  15.1 0.0 copy-done.7
  15.1 1.1 %tables.1 = (bf16[160,1024]{1,0:T(8,128)(2,1)S(1)}, bf16[160,1024]{1,0:T(8,128)(2,1)S(1)}, bf16[256,1024]{1,0:T(8,128)(2,1)S(1)}, bf16[256,256]{1,0:T(8,128)(2,1...) custom-call(s32[1,2]{1,0:T(1,128)S(1)} %copy-done.6, s32[32]{0:T(128)S(1)} %copy-done.7, ...), custom_call_target="tpu_custom_call" | custom-call | flops 100000000 | bytes 3000000 | tf_op jit(solution)/shard_map/tables/pallas_call | solution.py:349
  16.3 0.8 %copy-done.8 = bf16[256,1024]{1,0:T(8,128)(2,1)} copy-done((bf16[256,1024]{1,0:T(8,128)(2,1)}, bf16[256,1024]{1,0:T(8,128)(2,1)S(1)}, u32[]{:S(2)}) %copy-start.8) | copy-done | bytes 524312
  17.1 14.2 %all-to-all-done.received = bf16[32,64,128]{2,1,0:T(8,128)(2,1)S(1)} async-done(((bf16[32,64,128]{2,1,0:T(8,128)(2,1)}), bf16[32,64,128]{2,1,0:T(8,128)(2,1)S(1)}, u32[]{:S(2)}, u32[]{:S(2)}) %all-to-all-start) | async-done | bytes 524320 | tf_op jit(solution)/shard_map/all_to_all | solution.py:348
  31.3 0.4 project.1
  31.7 0.0 copy-start.10
  31.7 0.0 copy-start.11
  31.7 13.4 %all_to_all.15.mine = bf16[16,128,128]{2,1,0:T(8,128)(2,1)S(1)} all-to-all(bf16[16,128,128]{2,1,0:T(8,128)(2,1)S(1)} %project.1), channel_id=1, replica_groups={{0,32,1,33,128,160,129,161,256,288,257,289,384,416,385,417},{64,96,65,9..., dimensions={0} | all-to-all | bytes 1048576 | tf_op jit(solution)/shard_map/all_to_all | solution.py:373
  45.2 2.9 %collective-permute-start = (bf16[16,128,128]{2,1,0:T(8,128)(2,1)S(1)}, bf16[16,128,128]{2,1,0:T(8,128)(2,1)S(1)}, u32[]{:S(2)}, u32[]{:S(2)}) collective-permute-start(bf16[16,128,128]{2,1,0:T(8,128)(2,1)S(1)} %all_to_all.15.mine), channel_id=1, source_target_pairs={{0,16},{16,0},{32,48},{48,32},{64,80},{80,64},{96,112},{112,96},{1... | collective-permute-start | bytes 1572872 | tf_op jit(solution)/shard_map/ppermute | solution.py:400
  48.1 1.5 %before.1 = (bf16[512,256]{1,0:T(8,128)(2,1)S(1)}, f32[512,128]{1,0:T(8,128)S(1)}, f32[512,128]{1,0:T(8,128)S(1)}, bf16[256,128]{1,0:T(8,128)(2,1)S(1)}, f32[3,2...) custom-call(bf16[32,64,128]{2,1,0:T(8,128)(2,1)S(1)} %all-to-all-don, ...), custom_call_target="tpu_custom_call" | custom-call | flops 1000000000 | bytes 6000000 | tf_op jit(solution)/shard_map/before/pallas_call | solution.py:381
  49.6 0.0 collective-permute-done.other
  49.6 5.1 %passes.1 = bf16[32,16,128]{2,1,0:T(8,128)(2,1)S(1)} custom-call(bf16[16,128,128]{2,1,0:T(8,128)(2,1)S(1)} %collective-permute-done.other, bf16[256,1024]{1,0:T(8,128)(2,1)S(1)} %copy-done.9, bf16[256,256]{1,0:T(8,128)(2,1)S(1)} %get-tuple-element.26.residual, f32[256,256]{1,0:T(8,128)S(1)} %get-tuple-element.27.mask, ...), custom_call_target="tpu_custom_call" | custom-call | flops 5000000000 | bytes 4000000 | tf_op jit(solution)/shard_map/passes/pallas_call | solution.py:401
  54.7 12.6 %all_to_all.16 = bf16[32,16,128]{2,1,0:T(8,128)(2,1)S(1)} all-to-all(bf16[32,16,128]{2,1,0:T(8,128)(2,1)S(1)} %passes.1), channel_id=1, replica_groups=mesh['frame'=32,'batch'=16] {'frame'}, dimensions={0} | all-to-all | bytes 262144 | tf_op jit(solution)/shard_map/all_to_all | solution.py:413
  67.3 0.7 %convert_add_fusion = f32[512,128]{1,0:T(8,128)} fusion(f32[512,128]{1,0:T(8,128)S(1)} %get-tuple-element.22, bf16[32,16,128]{2,1,0:T(8,128)(2,1)S(1)} %all_to_all.16), kind=kLoop, calls=%fused_computation | loop fusion | flops 131072 | bytes 655360 | tf_op jit(solution)/shard_map/add | solution.py:414
  (12 shorter events, 0.0 us)
Async XLA Ops:
  0.0 14.5 %copy-start.2 = (bf16[128,1024]{1,0:T(8,128)(2,1)S(1)}, bf16[128,1024]{1,0:T(8,128)(2,1)}, u32[]{:S(2)}) copy-start(bf16[128,1024]{1,0:T(8,128)(2,1)} %w_in.1) | copy-start | bytes 786436
  0.0 14.5 %copy-start.3 = (bf16[1024,128]{1,0:T(8,128)(2,1)S(1)}, bf16[1024,128]{1,0:T(8,128)(2,1)}, u32[]{:S(2)}) copy-start(bf16[1024,128]{1,0:T(8,128)(2,1)} %w_res.1) | copy-start | bytes 786436
  0.0 14.5 %copy-start.4 = (bf16[32,256]{1,0:T(8,128)(2,1)S(1)}, bf16[32,256]{1,0:T(8,128)(2,1)}, u32[]{:S(2)}) copy-start(bf16[32,256]{1,0:T(8,128)(2,1)} %constant.4.feats) | copy-start | bytes 49156
  0.0 14.5 %copy-start.5 = (f32[1024]{0:T(1024)S(1)}, f32[1024]{0:T(1024)}, u32[]{:S(2)}) copy-start(f32[1024]{0:T(1024)} %param.19) | copy-start | bytes 12292
  2.9 11.6 %copy-start = (f32[512,2,128]{2,1,0:T(2,128)S(1)}, f32[512,2,128]{2,1,0:T(2,128)}, u32[]{:S(2)}) copy-start(f32[512,2,128]{2,1,0:T(2,128)} %param.13) | copy-start | bytes 1572868
  2.9 11.6 %copy-start.1 = (bf16[256,1024]{1,0:T(8,128)(2,1)S(1)}, bf16[256,1024]{1,0:T(8,128)(2,1)}, u32[]{:S(2)}) copy-start(bf16[256,1024]{1,0:T(8,128)(2,1)} %w_level.1) | copy-start | bytes 1572868
  2.9 28.3 %all-to-all-start = ((bf16[32,64,128]{2,1,0:T(8,128)(2,1)}), bf16[32,64,128]{2,1,0:T(8,128)(2,1)S(1)}, u32[]{:S(2)}, u32[]{:S(2)}) async-start(bf16[32,64,128]{2,1,0:T(8,128)(2,1)} %pack.1), calls=%async_computation | async-start | bytes 1048576 | tf_op jit(solution)/shard_map/all_to_all | solution.py:348
  14.5 0.7 copy-start.6
  14.5 0.7 copy-start.7
  16.3 0.8 %copy-start.8 = (bf16[256,1024]{1,0:T(8,128)(2,1)}, bf16[256,1024]{1,0:T(8,128)(2,1)S(1)}, u32[]{:S(2)}) copy-start(bf16[256,1024]{1,0:T(8,128)(2,1)S(1)} %get-tuple-element.25.embed_in) | copy-start | bytes 1572868
  31.7 16.3 %copy-start.9 = (bf16[256,1024]{1,0:T(8,128)(2,1)S(1)}, bf16[256,1024]{1,0:T(8,128)(2,1)}, u32[]{:S(2)}) copy-start(bf16[256,1024]{1,0:T(8,128)(2,1)} %copy-done.8) | copy-start | bytes 1572868
  31.7 16.3 %copy-start.10 = (bf16[1024,128]{1,0:T(8,128)(2,1)S(1)}, bf16[1024,128]{1,0:T(8,128)(2,1)}, u32[]{:S(2)}) copy-start(bf16[1024,128]{1,0:T(8,128)(2,1)} %w_out.1) | copy-start | bytes 786436
  31.7 16.3 %copy-start.11 = (f32[512,128]{1,0:T(8,128)S(1)}, f32[512,128]{1,0:T(8,128)}, u32[]{:S(2)}) copy-start(f32[512,128]{1,0:T(8,128)} %fresh.1) | copy-start | bytes 786436
  45.2 4.4 %collective-permute-start = (bf16[16,128,128]{2,1,0:T(8,128)(2,1)S(1)}, bf16[16,128,128]{2,1,0:T(8,128)(2,1)S(1)}, u32[]{:S(2)}, u32[]{:S(2)}) collective-permute-start(bf16[16,128,128]{2,1,0:T(8,128)(2,1)S(1)} %all_to_all.15.mine), channel_id=1, source_target_pairs={{0,16},{16,0},{32,48},{48,32},{64,80},{80,64},{96,112},{112,96},{1... | collective-permute-start | bytes 1572872 | tf_op jit(solution)/shard_map/ppermute | solution.py:400

commit v5 on v4

--- a/solution.py
+++ b/solution.py
@@ -48,14 +48,21 @@
     return lax.broadcasted_iota(jnp.int32, shape, dim)
 
 
-def pack_kernel(levels, window_in, noise_in, w_qkv_in, out, window, noise, w_qkv, sems):
+def pack_kernel(levels, window_in, noise_in, w_qkv_in, out, window, noise, w_qkv, weights, states, sems):
     copies = [
         pltpu.make_async_copy(src, dst, sems.at[k])
         for k, (src, dst) in enumerate(
-            [(w_qkv_in, w_qkv), (window_in, window), (noise_in, noise)]
+            [
+                (w_qkv_in, w_qkv),
+                (window_in, window),
+                (noise_in, noise),
+                (weights, out.at[:, 0:32]),
+                (states.at[0], out.at[:, 32:48]),
+                (states.at[1], out.at[:, 48:64]),
+            ]
         )
     ]
-    for copy in copies:
+    for copy in copies[:3]:
         copy.start()
     first = jnp.full((8, C), levels[0, 0], jnp.int32).astype(F32)
     second = jnp.full((8, C), levels[0, 1], jnp.int32).astype(F32)
@@ -82,14 +89,19 @@
             piece = jnp.where(lane == 96, first[:1], jnp.where(lane == 97, second[:1], piece))
             piece = piece.astype(BF16)
             for z in (i, i + 2):
-                out[h // 2 * 8 + z * 2 + h % 2, 0:32, :] = piece
+                weights[h // 2 * 8 + z * 2 + h % 2] = piece
+    copies[3].start()
     copies[1].wait()
     state = window[...]
     scaled = state / jnp.sqrt(1.0 + sigma * sigma)
-    out[:, 32:48, :] = scaled.reshape(FRAMES, POS, C).astype(BF16)
+    states[0] = scaled.reshape(FRAMES, POS, C).astype(BF16)
+    copies[4].start()
     copies[2].wait()
     base = state + (0.6 * sigma_of(first + 1.0)[:1]) * noise[pl.ds(0, ROWS, stride=2), :]
-    out[:, 48:64, :] = base.reshape(FRAMES, POS, C).astype(BF16)
+    states[1] = base.reshape(FRAMES, POS, C).astype(BF16)
+    copies[5].start()
+    for copy in copies[3:]:
+        copy.wait()
 
 
 def split(value):
@@ -99,7 +111,7 @@
 
 def table_kernel(
     levels, reach, feats, w_level, w_in, gain, w_res, noise,
-    high, low, embed_in, residual, mask, late,
+    high, low, embed_in, residual, mask, late, odd_rows,
 ):
     emb = dot(feats[...], w_level[...])
     embed_in[0:128, :] = w_in[...]
@@ -120,7 +132,8 @@
     )
     mask[...] = jnp.where(allowed, F32(0.0), F32(-1e30))
     level = jnp.full((8, C), levels[0, 1], jnp.int32).astype(F32)[:1]
-    late[...] = (0.6 * sigma_of(level + 1.0)) * noise[pl.ds(1, ROWS, stride=2), :]
+    odd_rows[...] = pltpu.roll(noise[...], 2 * ROWS - 1, 0)
+    late[...] = (0.6 * sigma_of(level + 1.0)) * odd_rows[pl.ds(0, ROWS, stride=2), :]
 
 
 def project_kernel(received, high, low, out):
@@ -313,13 +326,13 @@
     ]
 
 
-def call(kernel, name, out_shape, in_specs, cost, scratch_shapes=(), limit=LIMIT):
+def call(kernel, name, out_shape, in_specs, cost, scratch_shapes=(), limit=LIMIT, outputs=VMEM):
     flops, bytes_accessed = cost
     return pl.pallas_call(
         kernel,
         out_shape=out_shape,
         in_specs=in_specs,
-        out_specs=jax.tree.map(lambda _: VMEM, out_shape),
+        out_specs=jax.tree.map(lambda _: outputs, out_shape),
         scratch_shapes=scratch_shapes,
         compiler_params=pltpu.CompilerParams(vmem_limit_bytes=limit),
         cost_estimate=pl.CostEstimate(
@@ -341,9 +354,12 @@
             pltpu.VMEM((ROWS, C), F32),
             pltpu.VMEM((2 * ROWS, C), F32),
             pltpu.VMEM((D // FRAMES, 3 * D), BF16),
-            pltpu.SemaphoreType.DMA((3,)),
+            pltpu.VMEM((FRAMES, 32, C), BF16),
+            pltpu.VMEM((2, FRAMES, POS, C), BF16),
+            pltpu.SemaphoreType.DMA((6,)),
         ],
         None,
+        HBM,
     )(levels, window, pairs_of_noise, w_qkv)
     received = lax.all_to_all(payload, "frame", split_axis=0, concat_axis=0, tiled=True)
     high, low, embed_in, residual, mask, late = call(
@@ -359,6 +375,7 @@
         ),
         [SMEM, SMEM] + [VMEM] * 6,
         (10**8, 3 * 10**6),
+        [pltpu.VMEM((2 * ROWS, C), F32)],
     )(
         levels, reach, feats_table(), w_level, w_in, norm_gain.reshape(1, D), w_res,
         pairs_of_noise,

time: 68.4 us -> 68.3 us (level)
  no operation moved by 1% of the time
where the time goes in v5:
time: 68.3 us; the launch traced here: 67.9 us
  blocking collectives  26 us (38%)
  starting transfers between devices  14.4 us (21%)
  waiting for transfers between devices  14.1 us (21%)
  Pallas kernels  11.1 us (16%)
  local copies, waits for them, and re-layouts  1.44 us (2%)
  other arithmetic  0.73 us (1%)
    all_to_all x1, waiting for transfers between devices, on_device(): lax.all_to_all(payload, 'frame', split_axis=0, concat_axis=0, tiled=True)  14.1 us
    all_to_all x1, blocking collectives, on_device(): lax.all_to_all(packed, ('frame', 'batch'), split_axis=0, concat_axis=0, t...  13.4 us
    all_to_all x1, blocking collectives, on_device(): lax.all_to_all(state, 'frame', split_axis=0, concat_axis=0, tiled=True)  12.6 us
    all_to_all x1, starting transfers between devices, on_device(): lax.all_to_all(payload, 'frame', split_axis=0, concat_axis=0, tiled=True)  11.5 us
    pallas_call x1, Pallas kernels, on_device(): call(passes_kernel, 'passes', struct((FRAMES, POS, C), BF16), [VMEM] * 15...  5.11 us
    ppermute x1, starting transfers between devices, on_device(): other = lax.ppermute(mine, 'frame', [(i, i ^ 1) for i in range(FRAMES)])  2.85 us
    pallas_call x1, Pallas kernels, on_device(): call(pack_kernel, 'pack', struct((FRAMES, 64, C), BF16), [SMEM] + [HBM] *...  2.8 us
    pallas_call x1, Pallas kernels, on_device(): call(before_kernel, 'before', (struct((ROWS, 2 * C), BF16), struct((ROWS,...  1.51 us
  transfers between devices with their start and end apart: 2, of which 1 were waited for; matrix products, arithmetic and copies ran while one was open for 0% of the time, Pallas kernels for 4%

profile of v5, /device:TPU:1, one launch (start us, length us, event | category | flops | bytes accessed | tf_op | source)
XLA Modules:
  0.0 67.9 jit_solution(7179758207460901253)
XLA Ops:
  0.0 0.0 copy-start.5
  0.0 2.8 %pack.1 = bf16[32,64,128]{2,1,0:T(8,128)(2,1)} custom-call(s32[1,2]{1,0:T(1,128)} %levels.3, f32[512,128]{1,0:T(8,128)} %window_in.1, f32[1024,128]{1,0:T(8,128)} %bitcast.5, bf16[32,3072]{1,0:T(8,128)(2,1)} %w_qkv_in.1), custom_call_target="tpu_custom_call" | custom-call | flops 100000000 | bytes 2000000 | tf_op jit(solution)/shard_map/pack/pallas_call | solution.py:347
  2.8 0.0 copy-start
  2.8 0.0 copy-start.1
  2.9 11.5 %all-to-all-start = ((bf16[32,64,128]{2,1,0:T(8,128)(2,1)}), bf16[32,64,128]{2,1,0:T(8,128)(2,1)S(1)}, u32[]{:S(2)}, u32[]{:S(2)}) async-start(bf16[32,64,128]{2,1,0:T(8,128)(2,1)} %pack.1), calls=%async_computation | async-start | bytes 1048576 | tf_op jit(solution)/shard_map/all_to_all | solution.py:364
  14.4 0.0 copy-start.6
  14.4 0.0 copy-start.7
  14.4 0.0 copy-done.2
  14.5 0.6 copy-done.6
  15.1 0.0 copy-done.7
  15.1 1.2 %tables.1 = (bf16[160,1024]{1,0:T(8,128)(2,1)S(1)}, bf16[160,1024]{1,0:T(8,128)(2,1)S(1)}, bf16[256,1024]{1,0:T(8,128)(2,1)S(1)}, bf16[256,256]{1,0:T(8,128)(2,1...) custom-call(s32[1,2]{1,0:T(1,128)S(1)} %copy-done.6, s32[32]{0:T(128)S(1)} %copy-done.7, ...), custom_call_target="tpu_custom_call" | custom-call | flops 100000000 | bytes 3000000 | tf_op jit(solution)/shard_map/tables/pallas_call | solution.py:365
  16.3 0.0 copy-start.8
  16.3 0.8 %copy-done.8 = bf16[256,1024]{1,0:T(8,128)(2,1)} copy-done((bf16[256,1024]{1,0:T(8,128)(2,1)}, bf16[256,1024]{1,0:T(8,128)(2,1)S(1)}, u32[]{:S(2)}) %copy-start.8) | copy-done | bytes 524312
  17.1 14.1 %all-to-all-done.received = bf16[32,64,128]{2,1,0:T(8,128)(2,1)S(1)} async-done(((bf16[32,64,128]{2,1,0:T(8,128)(2,1)}), bf16[32,64,128]{2,1,0:T(8,128)(2,1)S(1)}, u32[]{:S(2)}, u32[]{:S(2)}) %all-to-all-start) | async-done | bytes 524320 | tf_op jit(solution)/shard_map/all_to_all | solution.py:364
  31.2 0.4 project.1
  31.6 0.0 copy-start.10
  31.7 0.0 copy-start.11
  31.7 13.4 %all_to_all.15.mine = bf16[16,128,128]{2,1,0:T(8,128)(2,1)S(1)} all-to-all(bf16[16,128,128]{2,1,0:T(8,128)(2,1)S(1)} %project.1), channel_id=1, replica_groups={{0,32,1,33,128,160,129,161,256,288,257,289,384,416,385,417},{64,96,65,9..., dimensions={0} | all-to-all | bytes 1048576 | tf_op jit(solution)/shard_map/all_to_all | solution.py:390
  45.1 2.9 %collective-permute-start = (bf16[16,128,128]{2,1,0:T(8,128)(2,1)S(1)}, bf16[16,128,128]{2,1,0:T(8,128)(2,1)S(1)}, u32[]{:S(2)}, u32[]{:S(2)}) collective-permute-start(bf16[16,128,128]{2,1,0:T(8,128)(2,1)S(1)} %all_to_all.15.mine), channel_id=1, source_target_pairs={{0,16},{16,0},{32,48},{48,32},{64,80},{80,64},{96,112},{112,96},{1... | collective-permute-start | bytes 1572872 | tf_op jit(solution)/shard_map/ppermute | solution.py:417
  48.0 1.5 %before.1 = (bf16[512,256]{1,0:T(8,128)(2,1)S(1)}, f32[512,128]{1,0:T(8,128)S(1)}, f32[512,128]{1,0:T(8,128)S(1)}, bf16[256,128]{1,0:T(8,128)(2,1)S(1)}, f32[3,2...) custom-call(bf16[32,64,128]{2,1,0:T(8,128)(2,1)S(1)} %all-to-all-don, ...), custom_call_target="tpu_custom_call" | custom-call | flops 1000000000 | bytes 6000000 | tf_op jit(solution)/shard_map/before/pallas_call | solution.py:398
  49.5 0.0 collective-permute-done.other
  49.5 5.1 %passes.1 = bf16[32,16,128]{2,1,0:T(8,128)(2,1)S(1)} custom-call(bf16[16,128,128]{2,1,0:T(8,128)(2,1)S(1)} %collective-permute-done.other, bf16[256,1024]{1,0:T(8,128)(2,1)S(1)} %copy-done.9, bf16[256,256]{1,0:T(8,128)(2,1)S(1)} %get-tuple-element.26.residual, f32[256,256]{1,0:T(8,128)S(1)} %get-tuple-element.27.mask, ...), custom_call_target="tpu_custom_call" | custom-call | flops 5000000000 | bytes 4000000 | tf_op jit(solution)/shard_map/passes/pallas_call | solution.py:418
  54.6 12.6 %all_to_all.16 = bf16[32,16,128]{2,1,0:T(8,128)(2,1)S(1)} all-to-all(bf16[32,16,128]{2,1,0:T(8,128)(2,1)S(1)} %passes.1), channel_id=1, replica_groups=mesh['frame'=32,'batch'=16] {'frame'}, dimensions={0} | all-to-all | bytes 262144 | tf_op jit(solution)/shard_map/all_to_all | solution.py:430
  67.2 0.7 %convert_add_fusion = f32[512,128]{1,0:T(8,128)} fusion(f32[512,128]{1,0:T(8,128)S(1)} %get-tuple-element.22, bf16[32,16,128]{2,1,0:T(8,128)(2,1)S(1)} %all_to_all.16), kind=kLoop, calls=%fused_computation | loop fusion | flops 131072 | bytes 655360 | tf_op jit(solution)/shard_map/add | solution.py:431
  (12 shorter events, 0.0 us)
Async XLA Ops:
  0.0 14.4 %copy-start.2 = (bf16[128,1024]{1,0:T(8,128)(2,1)S(1)}, bf16[128,1024]{1,0:T(8,128)(2,1)}, u32[]{:S(2)}) copy-start(bf16[128,1024]{1,0:T(8,128)(2,1)} %w_in.1) | copy-start | bytes 786436
  0.0 14.4 %copy-start.3 = (bf16[1024,128]{1,0:T(8,128)(2,1)S(1)}, bf16[1024,128]{1,0:T(8,128)(2,1)}, u32[]{:S(2)}) copy-start(bf16[1024,128]{1,0:T(8,128)(2,1)} %w_res.1) | copy-start | bytes 786436
  0.0 14.4 %copy-start.4 = (bf16[32,256]{1,0:T(8,128)(2,1)S(1)}, bf16[32,256]{1,0:T(8,128)(2,1)}, u32[]{:S(2)}) copy-start(bf16[32,256]{1,0:T(8,128)(2,1)} %constant.4.feats) | copy-start | bytes 49156
  0.0 14.4 %copy-start.5 = (f32[1024]{0:T(1024)S(1)}, f32[1024]{0:T(1024)}, u32[]{:S(2)}) copy-start(f32[1024]{0:T(1024)} %param.19) | copy-start | bytes 12292
  2.8 11.6 %copy-start = (f32[512,2,128]{2,1,0:T(2,128)S(1)}, f32[512,2,128]{2,1,0:T(2,128)}, u32[]{:S(2)}) copy-start(f32[512,2,128]{2,1,0:T(2,128)} %param.13) | copy-start | bytes 1572868
  2.8 11.6 %copy-start.1 = (bf16[256,1024]{1,0:T(8,128)(2,1)S(1)}, bf16[256,1024]{1,0:T(8,128)(2,1)}, u32[]{:S(2)}) copy-start(bf16[256,1024]{1,0:T(8,128)(2,1)} %w_level.1) | copy-start | bytes 1572868
  2.9 28.3 %all-to-all-start = ((bf16[32,64,128]{2,1,0:T(8,128)(2,1)}), bf16[32,64,128]{2,1,0:T(8,128)(2,1)S(1)}, u32[]{:S(2)}, u32[]{:S(2)}) async-start(bf16[32,64,128]{2,1,0:T(8,128)(2,1)} %pack.1), calls=%async_computation | async-start | bytes 1048576 | tf_op jit(solution)/shard_map/all_to_all | solution.py:364
  14.4 0.7 copy-start.6
  14.4 0.7 copy-start.7
  16.3 0.8 %copy-start.8 = (bf16[256,1024]{1,0:T(8,128)(2,1)}, bf16[256,1024]{1,0:T(8,128)(2,1)S(1)}, u32[]{:S(2)}) copy-start(bf16[256,1024]{1,0:T(8,128)(2,1)S(1)} %get-tuple-element.25.embed_in) | copy-start | bytes 1572868
  31.6 16.3 %copy-start.9 = (bf16[256,1024]{1,0:T(8,128)(2,1)S(1)}, bf16[256,1024]{1,0:T(8,128)(2,1)}, u32[]{:S(2)}) copy-start(bf16[256,1024]{1,0:T(8,128)(2,1)} %copy-done.8) | copy-start | bytes 1572868
  31.6 16.3 %copy-start.10 = (bf16[1024,128]{1,0:T(8,128)(2,1)S(1)}, bf16[1024,128]{1,0:T(8,128)(2,1)}, u32[]{:S(2)}) copy-start(bf16[1024,128]{1,0:T(8,128)(2,1)} %w_out.1) | copy-start | bytes 786436
  31.7 16.3 %copy-start.11 = (f32[512,128]{1,0:T(8,128)S(1)}, f32[512,128]{1,0:T(8,128)}, u32[]{:S(2)}) copy-start(f32[512,128]{1,0:T(8,128)} %fresh.1) | copy-start | bytes 786436
  45.1 4.4 %collective-permute-start = (bf16[16,128,128]{2,1,0:T(8,128)(2,1)S(1)}, bf16[16,128,128]{2,1,0:T(8,128)(2,1)S(1)}, u32[]{:S(2)}, u32[]{:S(2)}) collective-permute-start(bf16[16,128,128]{2,1,0:T(8,128)(2,1)S(1)} %all_to_all.15.mine), channel_id=1, source_target_pairs={{0,16},{16,0},{32,48},{48,32},{64,80},{80,64},{96,112},{112,96},{1... | collective-permute-start | bytes 1572872 | tf_op jit(solution)/shard_map/ppermute | solution.py:417
